TPU v7x, 32 devices: a whole 2x2x4 slice. The times are simulated.
32 devices in a mesh: seq: 8 (over z, y), head: 4 (over x, core).
Axes of the slice: x: 2, y: 2, z: 4, core: 2. Of those that a mesh axis runs over, the one named last changes fastest.
Arguments:
- queries: bfloat16 [4096, 4096], P('seq', 'head'), may hold values from -8 to 8
- keys: bfloat16 [4096, 4096], P('seq', 'head'), may hold values from -8 to 8
- values: bfloat16 [4096, 4096], P('seq', 'head'), may hold values from -6 to 6
- w_out: bfloat16 [4096, 4096], P('head', 'seq'), may hold values from -0.125 to 0.125
- grad_y: bfloat16 [4096, 4096], P('seq', 'head'), may hold values from -6 to 6
Outputs:
- mixer_result: bfloat16 [4096, 4096], P('seq', 'head')
- grad_queries: bfloat16 [4096, 4096], P('seq', 'head')
- grad_keys: bfloat16 [4096, 4096], P('seq', 'head')
- grad_values: bfloat16 [4096, 4096], P('seq', 'head')
- projection_sensitivity: float32 [4096, 4096], P('head', 'seq')
All inputs are finite; a program needn't handle non-finite values.
Results may differ from a plain program's by a relative error of at most 0.025.
Values may be sent and summed in bfloat16 or wider, within the bound.
A program may use at most 128 MiB of HBM per device.

v0:
```python
import math

import jax
import jax.numpy as jnp
from jax import lax
from jax.sharding import PartitionSpec as P

DH = 128
BLOCK = 64
BAND = 8


EPSILON = 1e-05
MASKED = -1e30


def entering(shard, axis, join, neutral, backward):
    count = lax.axis_size(axis)
    place = lax.axis_index(axis)
    ahead = count - 1 - place if backward else place
    gathered = lax.all_gather(shard.astype(jnp.bfloat16), axis)
    state = jnp.zeros_like(shard) + jnp.asarray(neutral, shard.dtype)

    def one(turn, state):
        source = count - 1 - turn if backward else turn
        return join(state, lax.dynamic_index_in_dim(gathered, source, 0, False).astype(shard.dtype))

    return lax.fori_loop(0, ahead, one, state)


def shifted(shard, axis, by):
    count = lax.axis_size(axis)
    pairs = [(i, i + by) for i in range(count) if 0 <= i + by < count]
    return lax.ppermute(shard, axis, pairs)


def band_allowed(first, rows, span, offset):
    query = first + jnp.arange(rows, dtype=jnp.int32)
    place = first - (BAND - 1) * BLOCK + jnp.arange(span, dtype=jnp.int32)
    near = place[:, None] // BLOCK >= query[None, :] // BLOCK - (BAND - 1)
    return (place[:, None] <= query[None, :]) & near & (place[:, None] + offset >= 0)


def add_states(earlier, later):
    return earlier + later


def carry_states(local_sum, backward):
    return entering(local_sum, "seq", add_states, jnp.zeros_like(local_sum), backward)


def shards(queries, keys, values, w_out, grad_y):
    tok_rows, width = queries.shape
    groups = width // DH
    block_count = tok_rows // BLOCK
    rows = BAND * BLOCK
    edge = (BAND - 1) * BLOCK
    span = rows + edge
    query_blocks = tok_rows // rows
    score_scale = 1.0 / math.sqrt(DH)
    offset = lax.axis_index("seq") * tok_rows
    tokens_all = tok_rows * lax.axis_size("seq")
    query_block_rows = queries.reshape(block_count, BLOCK, groups, DH)
    lookup_tile_entries = keys.reshape(block_count, BLOCK, groups, DH)
    value_block_rows = values.reshape(block_count, BLOCK, groups, DH)
    cross_block_totals = jnp.einsum(
        "nbhk,nbhv->nhkv", lookup_tile_entries, value_block_rows, preferred_element_type=jnp.float32
    )
    before = carry_states(jnp.sum(cross_block_totals, axis=0), False)
    running_state = (
        before[None] + jnp.cumsum(cross_block_totals, axis=0) - cross_block_totals
    ).astype(jnp.bfloat16)
    causal = (jnp.arange(BLOCK)[:, None] >= jnp.arange(BLOCK)[None, :])[None, None]
    inside_block_scores = jnp.where(
        causal,
        jnp.einsum(
            "nthk,njhk->nhtj",
            query_block_rows,
            lookup_tile_entries,
            preferred_element_type=jnp.float32,
        ),
        0.0,
    ).astype(jnp.bfloat16)
    linear_branch = jnp.einsum(
        "nthk,nhkv->nthv", query_block_rows, running_state, preferred_element_type=jnp.float32
    )
    linear_branch = linear_branch + jnp.einsum(
        "nhtj,njhv->nthv", inside_block_scores, value_block_rows, preferred_element_type=jnp.float32
    )
    linear_branch = linear_branch.reshape(tok_rows, groups, DH)
    inv_rms = lax.rsqrt(jnp.mean(linear_branch * linear_branch, axis=-1, keepdims=True) + EPSILON)
    normed = linear_branch * inv_rms
    edge_pair = shifted(jnp.stack([keys[tok_rows - edge :], values[tok_rows - edge :]]), "seq", 1)
    lookup_matrix_padded = jnp.concatenate([edge_pair[0], keys]).reshape(
        tok_rows + edge, groups, DH
    )
    values_wide = jnp.concatenate([edge_pair[1], values]).reshape(tok_rows + edge, groups, DH)
    q_heads = queries.reshape(tok_rows, groups, DH)

    def band_scores(first, q_rows, k_span):
        score = (
            jnp.einsum("khd,qhd->hkq", k_span, q_rows, preferred_element_type=jnp.float32)
            * score_scale
        )
        return jnp.where(band_allowed(first, rows, span, offset)[None], score, MASKED)

    def window_block(index):
        first = index * rows
        score = band_scores(first, q_heads, lookup_matrix_padded)
        row_max = jnp.max(score, axis=1)
        raised = jnp.exp(score - row_max[:, None, :])
        inv_total = 1.0 / jnp.sum(raised, axis=1)
        probs = (raised * inv_total[:, None, :]).astype(jnp.bfloat16)
        return (
            jnp.einsum("hkq,khd->qhd", probs, values_wide, preferred_element_type=jnp.float32),
            row_max,
            inv_total,
        )

    outs, maxima, inverses = lax.map(window_block, jnp.arange(query_blocks, dtype=jnp.int32))
    window = outs.reshape(tok_rows, groups, DH)
    mixed = (normed + window).astype(jnp.bfloat16).reshape(tok_rows, width)
    partial_value = jnp.dot(
        mixed, lax.all_gather(w_out, "seq", axis=1, tiled=True), preferred_element_type=jnp.float32
    )
    mixer_result = lax.psum_scatter(
        partial_value.astype(jnp.bfloat16), "head", scatter_dimension=1, tiled=True
    )
    grad_full = lax.all_gather(grad_y, "head", axis=1, tiled=True)
    columns = grad_full
    grad_mixed = lax.dot_general(
        columns,
        lax.all_gather(w_out, "seq", axis=1, tiled=True),
        (((1,), (1,)), ((), ())),
        preferred_element_type=jnp.float32,
    )
    grad_mixed = grad_mixed.astype(jnp.bfloat16)
    columns = grad_full
    weight_part = lax.psum_scatter(
        lax.dot_general(
            columns, mixed, (((0,), (0,)), ((), ())), preferred_element_type=jnp.float32
        ).astype(jnp.bfloat16),
        "seq",
        scatter_dimension=0,
        tiled=True,
    ).astype(jnp.float32)
    projection_sensitivity = weight_part.T * tokens_all ** (-0.5)
    grad_mix = grad_mixed.reshape(tok_rows, groups, DH)
    grad_f = grad_mix.astype(jnp.float32)
    delta = jnp.sum(grad_f * window, axis=-1)
    inner = jnp.mean(grad_f * normed, axis=-1, keepdims=True)
    grad_lin = (inv_rms * (grad_f - normed * inner)).astype(jnp.bfloat16)
    upstream_tile_entries = grad_lin.reshape(block_count, BLOCK, groups, DH)
    reverse_state_totals = jnp.einsum(
        "nthk,nthv->nhkv",
        query_block_rows,
        upstream_tile_entries,
        preferred_element_type=jnp.float32,
    )
    local_back = jnp.sum(reverse_state_totals, axis=0)
    later = carry_states(local_back, True)
    back_state = (later[None] + local_back[None] - jnp.cumsum(reverse_state_totals, axis=0)).astype(
        jnp.bfloat16
    )
    intra_grad = jnp.where(
        causal,
        jnp.einsum(
            "nthv,njhv->nhtj",
            upstream_tile_entries,
            value_block_rows,
            preferred_element_type=jnp.float32,
        ),
        0.0,
    ).astype(jnp.bfloat16)
    asking_plain_entries = jnp.einsum(
        "nthv,nhkv->nthk", upstream_tile_entries, running_state, preferred_element_type=jnp.float32
    )
    asking_plain_entries = asking_plain_entries + jnp.einsum(
        "nhtj,njhk->nthk", intra_grad, lookup_tile_entries, preferred_element_type=jnp.float32
    )
    key_linear_rows = jnp.einsum(
        "njhv,nhkv->njhk", value_block_rows, back_state, preferred_element_type=jnp.float32
    )
    key_linear_rows = key_linear_rows + jnp.einsum(
        "nhtj,nthk->njhk", intra_grad, query_block_rows, preferred_element_type=jnp.float32
    )
    value_linear_rows = jnp.einsum(
        "njhk,nhkv->njhv", lookup_tile_entries, back_state, preferred_element_type=jnp.float32
    )
    value_linear_rows = value_linear_rows + jnp.einsum(
        "nhtj,nthv->njhv",
        inside_block_scores,
        upstream_tile_entries,
        preferred_element_type=jnp.float32,
    )

    def window_back(index, carry):
        q_acc, k_acc, v_acc = carry
        first = index * rows
        score = band_scores(first, q_heads, lookup_matrix_padded)
        probs = (jnp.exp(score - maxima[index][:, None, :]) * inverses[index][:, None, :]).astype(
            jnp.bfloat16
        )
        dprob = jnp.einsum(
            "khd,qhd->hkq", values_wide, grad_mix, preferred_element_type=jnp.float32
        )
        delta_rows = delta.T
        dscore = (
            probs.astype(jnp.float32) * (dprob - delta_rows[:, None, :]) * score_scale
        ).astype(jnp.bfloat16)
        q_acc = jnp.einsum(
            "hkq,khd->qhd", dscore, lookup_matrix_padded, preferred_element_type=jnp.float32
        )
        k_new = k_acc + jnp.einsum(
            "hkq,qhd->khd", dscore, q_heads, preferred_element_type=jnp.float32
        )
        v_new = v_acc + jnp.einsum(
            "hkq,qhd->khd", probs, grad_mix, preferred_element_type=jnp.float32
        )
        k_acc = k_new
        v_acc = v_new
        return (q_acc, k_acc, v_acc)

    start_carry = (
        jnp.zeros((tok_rows, groups, DH), jnp.float32),
        jnp.zeros((tok_rows + edge, groups, DH), jnp.float32),
        jnp.zeros((tok_rows + edge, groups, DH), jnp.float32),
    )
    q_window, k_wide_grad, v_wide_grad = lax.fori_loop(0, query_blocks, window_back, start_carry)
    returned = shifted(
        jnp.stack([k_wide_grad[:edge], v_wide_grad[:edge]]).astype(jnp.bfloat16), "seq", -1
    ).astype(jnp.float32)
    k_window = k_wide_grad[edge:].at[tok_rows - edge :].add(returned[0])
    v_window = v_wide_grad[edge:].at[tok_rows - edge :].add(returned[1])
    grad_queries = (
        (asking_plain_entries.reshape(tok_rows, groups, DH) + q_window)
        .astype(jnp.bfloat16)
        .reshape(tok_rows, width)
    )
    grad_keys = (
        (key_linear_rows.reshape(tok_rows, groups, DH) + k_window)
        .astype(jnp.bfloat16)
        .reshape(tok_rows, width)
    )
    grad_values = (
        (value_linear_rows.reshape(tok_rows, groups, DH) + v_window)
        .astype(jnp.bfloat16)
        .reshape(tok_rows, width)
    )
    return (mixer_result, grad_queries, grad_keys, grad_values, projection_sensitivity)


def solution(mesh):
    placed = (
        P("seq", "head"),
        P("seq", "head"),
        P("seq", "head"),
        P("head", "seq"),
        P("seq", "head"),
    )
    return jax.shard_map(
        shards,
        mesh=mesh,
        in_specs=placed,
        out_specs=(
            P("seq", "head"),
            P("seq", "head"),
            P("seq", "head"),
            P("seq", "head"),
            P("head", "seq"),
        ),
        check_vma=False,
    )
```

profile of v0, /device:TPU:0, one launch (start us, length us, event | category | flops | bytes accessed | tf_op | source)
XLA Modules:
  0.0 554.0 jit_solution(15575338909451485833)
XLA Ops:
  9.1 3.6 fusion.62
  17.0 6.1 %collective-permute-start = (bf16[2,448,1024]{2,1,0:T(8,128)(2,1)}, bf16[2,448,1024]{2,1,0:T(8,128)(2,1)}, u32[]{:S(2)}, u32[]{:S(2)}) collective-permute-start(bf16[2,448,1024]{2,1,0:T(8,128)(2,1)} %pad_maximum_fusion.2), channel_id=1, source_target_pairs={{0,4},{4,8},{8,12},{12,16},{16,20},{20,24},{24,28},{1,5},{5,9},{9,... | collective-permute-start | bytes 5505032 | tf_op jit(solution)/shard_map/ppermute | solution.py:34
  36.5 39.0 %collective-permute-done = bf16[2,448,1024]{2,1,0:T(8,128)(2,1)} collective-permute-done((bf16[2,448,1024]{2,1,0:T(8,128)(2,1)}, bf16[2,448,1024]{2,1,0:T(8,128)(2,1)}, u32[]{:S(2)}, u32[]{:S(2)}) %collective-permute-start) | collective-permute-done | bytes 1835040 | tf_op jit(solution)/shard_map/ppermute | solution.py:34
  79.6 7.7 %fusion.23 = f32[8,960,512]{2,1,0:T(8,128)} fusion(bf16[512,8,128]{2,0,1:T(8,128)(2,1)S(1)} %copy-done.19, bf16[448,8,128]{2,0,1:T(8,128)(2,1)S(1)} %copy.90, bf16[512,1024]{1,0:T(8,128)(2,1)S(1)} %copy-done.18), kind=kOutput, calls=%fused_computation.60 | convolution fusion | flops 1010565120 | bytes 18743296 | tf_op jit(solution)/shard_map/while/body/eval_jaxpr/khd,qhd->hkq/dot_general | solution.py:102
  87.4 20.5 %fusion.61 = (f32[8,512]{1,0:T(8,128)S(1)}, f32[8,960,512]{2,1,0:T(8,128)}) fusion(f32[8,960,512]{2,1,0:T(8,128)} %fusion.23, pred[960,512]{1,0:T(8,128)(4,1)S(1)} %fusion.16), kind=kOutput, calls=%fused_computation.117 | output fusion | flops 23593920 | bytes 31965184 | tf_op jit(solution)/shard_map/while/body/eval_jaxpr/sub | solution.py:111
  107.8 8.9 %multiply_convert_fusion.1 = bf16[8,960,512]{2,1,0:T(8,128)(2,1)} fusion(f32[8,960,512]{2,1,0:T(8,128)} %get-tuple-element.211, f32[8,512]{1,0:T(8,128)S(1)} %broadcast_divide_fusion), kind=kLoop, calls=%fused_computation.4 | loop fusion | flops 7864320 | bytes 23609344 | tf_op jit(solution)/shard_map/while/body/eval_jaxpr/convert_element_type | solution.py:113
  117.0 4.7 subtract_convert_fusion.1
  125.6 3.0 copy.85
  128.6 118.8 %all-gather.7.cloned.1.call-done = bf16[1024,4096]{1,0:T(8,128)(2,1)} async-done(((bf16[1024,512]{1,0:T(8,128)(2,1)}), bf16[1024,4096]{1,0:T(8,128)(2,1)}) %all-gather.7.cloned.1.call-update) | async-done | bytes 8388624 | tf_op jit(solution)/shard_map/all_gather | solution.py:124
  247.5 10.2 %convolution_convert_fusion.1 = bf16[512,1024]{1,0:T(8,128)(2,1)} fusion(bf16[512,4096]{1,0:T(8,128)(2,1)} %all-gather.9.cloned.1.call-done, bf16[1024,4096]{1,0:T(8,128)(2,1)} %all-gather.7.cloned.1.call-done), kind=kOutput, calls=%fused_computation.59 | convolution fusion | flops 4295491584 | bytes 13631488 | tf_op jit(solution)/shard_map/dot_general | solution.py:131
  259.9 2.9 convert_bitcast_fusion.1
  262.8 6.4 %fusion.8 = (f32[512,8]{0,1:T(8,128)S(1)}, f32[512,8]{0,1:T(8,128)S(1)}, bf16[512,8,128]{0,2,1:T(8,128)(2,1)}) fusion(bf16[512,1024]{0,1:T(8,128)(2,1)S(1)} %copy-done.25, f32[512,8,128]{0,2,1:T(8,128)S(1)} %copy-done.33, f32[512,8]{0,1:T(8,128)S(1)} %rsqrt.13, bf16[8,960,512]{2,1,0:T(8,128)(2,1)} %multiply_convert_fusion.1, ...), kind=kOutput, calls=%fused_computation.21 | convolution fusion | flops 1014751232 | bytes 14073856 | tf_op jit(solution)/shard_map/while/body/eval_jaxpr/hkq,khd->qhd/dot_general | solution.py:115
  277.8 9.0 %convert_bitcast_fusion = bf16[4096,1024]{0,1:T(8,128)(2,1)} fusion(bf16[512,1024]{0,1:T(8,128)(2,1)S(1)} %bitcast.180, bf16[512,4096]{1,0:T(8,128)(2,1)} %all-gather.9.cloned.1.call-done), kind=kOutput, calls=%fused_computation.8 | convolution fusion | flops 4299161600 | bytes 13631488 | tf_op jit(solution)/shard_map/dot_general | solution.py:140
  286.9 9.6 %convolution_convert_fusion = bf16[512,4096]{1,0:T(8,128)(2,1)} fusion(bf16[512,1024]{0,1:T(8,128)(2,1)S(1)} %bitcast.181, bf16[1024,4096]{1,0:T(8,128)(2,1)} %all-gather.7.cloned.1.call-done), kind=kOutput, calls=%fused_computation.12 | convolution fusion | flops 4297064448 | bytes 13631488 | tf_op jit(solution)/shard_map/dot_general | solution.py:123
  296.5 6.8 %multiply_convert_fusion = bf16[8,960,512]{2,1,0:T(8,128)(2,1)S(1)} fusion(bf16[8,960,512]{2,1,0:T(8,128)(2,1)} %multiply_convert_fusion.1, bf16[512,8,128]{0,2,1:T(8,128)(2,1)} %bitcast.170, f32[8,512]{1,0:T(8,128)S(1)} %bitcast.182, bf16[512,8,128]{2,0,1:T(8,128)(2,1)} %copy.88, bf16[448,8,128]{2,0,1:T(8,128)(2,1)} %copy.87), kind=kOutput, calls=%fused_computation.3 | convolution fusion | flops 1030225920 | bytes 18759680 | tf_op jit(solution)/shard_map/while/body/eval_jaxpr/khd,qhd->hkq/dot_general | solution.py:204
  303.3 4.4 convolution_bitcast_fusion.1
  325.4 5.9 %fusion.10 = bf16[512,8,128]{0,2,1:T(8,128)(2,1)} fusion(f32[512,8,128]{0,2,1:T(8,128)S(1)} %copy.100, bf16[8,960,512]{2,1,0:T(8,128)(2,1)} %copy-done, bf16[512,8,128]{2,0,1:T(8,128)(2,1)S(1)} %copy-done.20, bf16[448,8,128]{2,0,1:T(8,128)(2,1)} %copy-done.24), kind=kOutput, calls=%fused_computation.26 | convolution fusion | flops 1011613696 | bytes 12976128 | tf_op jit(solution)/shard_map/while/body/eval_jaxpr/hkq,khd->qhd/dot_general | solution.py:211
  335.6 33.5 %collective-permute-done.1 = bf16[2,448,8,128]{3,1,2,0:T(8,128)(2,1)} collective-permute-done((bf16[2,448,8,128]{3,1,2,0:T(8,128)(2,1)}, bf16[2,448,8,128]{3,1,2,0:T(8,128)(2,1)}, u32[]{:S(2)}, u32[]{:S(2)}) %collective-permute-start.1) | collective-permute-done | bytes 1835040 | tf_op jit(solution)/shard_map/ppermute | solution.py:34
  371.0 3.2 fusion.18
  374.2 8.0 %while.17 = (s32[]{:T(128)}, f32[8,128,128]{2,1,0:T(8,128)S(1)}, s32[]{:T(128)}, bf16[8,8,128,128]{3,2,1,0:T(8,128)(2,1)}, s32[]{:T(128)}, /*index=5*/s32[]{:T(128)}, s32[]{:T(128)}, s32[]{:T(128)}) while((s32[]{:T(128)}, f32[8,128,128]{2,1,0:T(8,128)S(1)}, s32[]{:T(128)}, bf16[8,8,128,128]{3,2,1,0:T(8,128)(2,1)}, s32[]{:T(128)}, ...), condition=%wide.region_12.13_spmd, body=%wide.region_11.12_spmd.sunk | while | flops 262150 | bytes 1310855 | solution.py:28
  384.3 3.1 subtract_convert_fusion
  397.9 2.9 bitcast_add_fusion.1
  404.4 95.9 %reduce-scatter.5.cloned.1.call-done = bf16[512,1024]{0,1:T(8,128)(2,1)} async-done(((bf16[4096,1024]{0,1:T(8,128)(2,1)}), bf16[512,1024]{0,1:T(8,128)(2,1)}) %reduce-scatter.5.cloned.1.call-update) | async-done | bytes 1048592 | tf_op jit(solution)/shard_map/reduce_scatter | solution.py:139
  503.1 43.8 %reduce-scatter.3.cloned.1.call-done = bf16[512,1024]{1,0:T(8,128)(2,1)} async-done(((bf16[512,4096]{1,0:T(8,128)(2,1)}), bf16[512,1024]{1,0:T(8,128)(2,1)}) %reduce-scatter.3.cloned.1.call-update) | async-done | bytes 1048592 | tf_op jit(solution)/shard_map/reduce_scatter | solution.py:126
  (165 shorter events, 89.0 us)
Async XLA Ops:
  7.2 109.5 %all-gather.11.cloned.1.call-start = ((), (), s32[]{:S(2)}) async-start(), calls=%async_computation.6 | async-start | bytes 2359296 | tf_op jit(solution)/shard_map/all_gather | solution.py:21
  8.8 25.2 %copy-start.10 = (bf16[64,8,8,128]{3,2,1,0:T(8,128)(2,1)}, bf16[64,8,8,128]{3,2,1,0:T(8,128)(2,1)S(1)}, u32[]{:S(2)}) copy-start(bf16[64,8,8,128]{3,2,1,0:T(8,128)(2,1)S(1)} %copy.129) | copy-start | bytes 3145732
  9.1 25.6 %copy-start.7 = (bf16[64,8,8,128]{3,2,1,0:T(8,128)(2,1)}, bf16[64,8,8,128]{3,2,1,0:T(8,128)(2,1)S(1)}, u32[]{:S(2)}) copy-start(bf16[64,8,8,128]{3,2,1,0:T(8,128)(2,1)S(1)} %copy.130) | copy-start | bytes 3145732
  12.7 115.9 %all-gather.9.cloned.1.call-start = ((), (), s32[]{:S(2)}) async-start(), calls=%async_computation.4 | async-start | bytes 5242880 | tf_op jit(solution)/shard_map/all_gather | solution.py:129
  13.4 234.0 %all-gather.7.cloned.1.call-start = ((), (), s32[]{:S(2)}) async-start(), calls=%async_computation.2 | async-start | bytes 9437184 | tf_op jit(solution)/shard_map/all_gather | solution.py:124
  14.2 360.0 %all-gather.13.cloned.1.call-start = ((), (), s32[]{:S(2)}) async-start(), calls=%async_computation.7 | async-start | bytes 2359296 | tf_op jit(solution)/shard_map/all_gather | solution.py:21
  17.0 58.5 %collective-permute-start = (bf16[2,448,1024]{2,1,0:T(8,128)(2,1)}, bf16[2,448,1024]{2,1,0:T(8,128)(2,1)}, u32[]{:S(2)}, u32[]{:S(2)}) collective-permute-start(bf16[2,448,1024]{2,1,0:T(8,128)(2,1)} %pad_maximum_fusion.2), channel_id=1, source_target_pairs={{0,4},{4,8},{8,12},{12,16},{16,20},{20,24},{24,28},{1,5},{5,9},{9,... | collective-permute-start | bytes 5505032 | tf_op jit(solution)/shard_map/ppermute | solution.py:34
  28.1 244.6 %copy-start.13 = (bf16[64,8,8,128]{3,2,1,0:T(8,128)(2,1)}, bf16[64,8,8,128]{3,2,1,0:T(8,128)(2,1)S(1)}, u32[]{:S(2)}) copy-start(bf16[64,8,8,128]{3,2,1,0:T(8,128)(2,1)S(1)} %copy.128) | copy-start | bytes 3145732
  117.0 4.7 copy-start.23
  272.8 5.0 copy-start.34
  277.4 222.9 %reduce-scatter.5.cloned.1.call-start = ((), (), s32[]{:S(2)}) async-start(), calls=%async_computation.5 | async-start | bytes 9437184 | tf_op jit(solution)/shard_map/reduce_scatter | solution.py:139
  286.8 260.1 %reduce-scatter.3.cloned.1.call-start = ((), (), s32[]{:S(2)}) async-start(), calls=%async_computation.3 | async-start | bytes 5242880 | tf_op jit(solution)/shard_map/reduce_scatter | solution.py:126
  296.5 11.4 %slice-start = ((s8[7864320]{0:T(1024)(128)(4,1)}), s8[4194304]{0:T(1024)(128)(4,1)S(1)}, s32[]{:S(2)}) async-start(s8[7864320]{0:T(1024)(128)(4,1)} %bitcast.148), calls=%async_computation.8 | async-start | bytes 8388608
  303.2 4.4 copy-start
  303.3 5.2 slice-start.1
  307.6 8.4 %copy-start.1 = (f32[960,8,128]{2,0,1:T(8,128)}, f32[960,8,128]{2,0,1:T(8,128)S(1)}, u32[]{:S(2)}) copy-start(f32[960,8,128]{2,0,1:T(8,128)S(1)} %convolution_bitcast_fusion.1) | copy-start | bytes 11796484
  312.1 4.0 copy-start.3
  312.2 3.2 copy-start.8
  313.7 55.4 %collective-permute-start.1 = (bf16[2,448,8,128]{3,1,2,0:T(8,128)(2,1)}, bf16[2,448,8,128]{3,1,2,0:T(8,128)(2,1)}, u32[]{:S(2)}, u32[]{:S(2)}) collective-permute-start(bf16[2,448,8,128]{3,1,2,0:T(8,128)(2,1)} %pad_maximum_fusion.3), channel_id=1, source_target_pairs={{4,0},{8,4},{12,8},{16,12},{20,16},{24,20},{28,24},{5,1},{9,5},{13... | collective-permute-start | bytes 5505032 | tf_op jit(solution)/shard_map/ppermute | solution.py:34
  316.1 4.3 copy-start.31
  333.7 37.2 %copy-start.2 = (f32[960,8,128]{2,0,1:T(8,128)S(1)}, f32[960,8,128]{2,0,1:T(8,128)}, u32[]{:S(2)}) copy-start(f32[960,8,128]{2,0,1:T(8,128)} %copy-done.1) | copy-start | bytes 11796484
  335.6 35.4 %slice-start.2 = ((f32[960,8,128]{2,0,1:T(8,128)}), f32[512,8,128]{2,0,1:T(8,128)S(1)}, s32[]{:S(2)}) async-start(f32[960,8,128]{2,0,1:T(8,128)} %copy-done.1), calls=%async_computation.10 | async-start | bytes 4194304 | tf_op jit(solution)/shard_map/slice | solution.py:233
  374.2 9.0 %copy-start.28 = (f32[8,128,128]{1,2,0:T(8,128)S(1)}, f32[8,128,128]{1,2,0:T(8,128)}, u32[]{:S(2)}) copy-start(f32[8,128,128]{1,2,0:T(8,128)} %copy-done.27) | copy-start | bytes 1572868
  393.3 4.7 copy-start.9
  (22 other events, 46.8 us)
Sparse Core Ops, SparseCore 0:
  12.8 67.6 all-gather.10
  82.0 37.9 all-gather.8
  122.0 125.3 all-gather.6
  277.5 50.0 all-gather.12
  331.1 169.1 reduce-scatter.4
  503.4 43.4 reduce-scatter.2
where the time goes:
time: 564 us; the launch traced here: 554 us
  waiting for transfers between devices  332 us (59%)
  matrix products  81.1 us (14%)
  other arithmetic  65.1 us (12%)
  local copies, waits for them, and re-layouts  51.3 us (9%)
  between operations  15 us (3%)
  starting transfers between devices  8.45 us (1%)
    all_gather x1, waiting for transfers between devices, shards(): lax.all_gather(w_out, 'seq', axis=1, tiled=True)  119 us
    reduce_scatter x1, waiting for transfers between devices, shards(): lax.psum_scatter(lax.dot_general(columns, mixed, (((0,), (0,)), ((), ()))...  95.9 us
    ppermute x2, waiting for transfers between devices, shifted(): return lax.ppermute(shard, axis, pairs)  72.4 us
    reduce_scatter x1, waiting for transfers between devices, shards(): lax.psum_scatter(partial_value.astype(jnp.bfloat16), 'head', scatter_dime...  43.8 us
    unnamed x86, local copies, waits for them, and re-layouts  23.4 us
    sub x1, other arithmetic, window_block(): raised = jnp.exp(score - row_max[:, None, :])  20.5 us
  transfers between devices with their start and end apart: 8, of which 5 were waited for; matrix products, arithmetic and copies ran while one was open for 28% of the time, Pallas kernels for 0%

commit v1 on v0

v1 whole, which is shorter than its diff:
```python
import math

import jax
import jax.numpy as jnp
from jax import lax
from jax.experimental import pallas as pl
from jax.experimental.pallas import tpu as pltpu
from jax.sharding import PartitionSpec as P

DH = 128
BLOCK = 64
BAND = 8
TILE = 128
EDGE = (BAND - 1) * BLOCK
LEAD = BAND * BLOCK
SPAN = LEAD + TILE
EPSILON = 1e-05
MASKED = -1e30
SCALE = 1.0 / math.sqrt(DH)
LOG2E = 1.0 / math.log(2.0)
F32 = jnp.float32
BF16 = jnp.bfloat16


def mm(a, b):
    return jnp.dot(a, b, preferred_element_type=F32)


def mm_nt(a, b):
    return lax.dot_general(a, b, (((1,), (1,)), ((), ())), preferred_element_type=F32)


def widen(wide, edge_ref, own_ref):
    wide[0 : LEAD - EDGE, :] = jnp.zeros((LEAD - EDGE, DH), wide.dtype)
    wide[LEAD - EDGE : LEAD, :] = edge_ref[...]
    wide[LEAD:, :] = own_ref[...]


def causal_t():
    key = lax.broadcasted_iota(jnp.int32, (TILE, TILE), 0)
    query = lax.broadcasted_iota(jnp.int32, (TILE, TILE), 1)
    return key <= query


def forward_kernel(
    first_ref, q_ref, k_ref, v_ref, ke_ref, ve_ref, before_ref,
    mixed_ref, probs_ref, win_ref, norm_ref, inv_ref, state_ref,
    kw, vw,
):
    tiles = q_ref.shape[0] // TILE
    widen(kw, ke_ref, k_ref)
    widen(vw, ve_ref, v_ref)
    vt = vw[...].T
    first = first_ref[0]
    key = lax.broadcasted_iota(jnp.int32, (SPAN, TILE), 0)
    query = lax.broadcasted_iota(jnp.int32, (SPAN, TILE), 1)
    low = (query // BLOCK + 1) * BLOCK
    high = query + LEAD
    causal = causal_t()
    state = before_ref[0]
    for i in range(tiles):
        rows = slice(i * TILE, (i + 1) * TILE)
        q = q_ref[rows, :]
        raw = mm_nt(kw[i * TILE : i * TILE + SPAN, :], q)
        allowed = (key >= jnp.maximum(low, LEAD - i * TILE - first)) & (key <= high)
        score = jnp.where(allowed, raw, MASKED)
        row_max = jnp.max(score, axis=0, keepdims=True)
        raised = jnp.exp2((score - row_max) * (SCALE * LOG2E))
        inv_total = 1.0 / jnp.sum(raised, axis=0, keepdims=True)
        probs = (raised * inv_total).astype(BF16)
        probs_ref[0, i] = probs
        window = mm(vt[:, i * TILE : i * TILE + SPAN], probs)
        vt_own = vt[:, LEAD + i * TILE : LEAD + (i + 1) * TILE]
        intra = jnp.where(causal, raw[LEAD:], 0.0).astype(BF16)
        rounded = state.astype(BF16)
        state_ref[0, i] = rounded
        linear = mm(vt_own, intra) + mm_nt(rounded, q)
        state = state + mm(vt_own, k_ref[rows, :])
        inv = lax.rsqrt(jnp.mean(linear * linear, axis=0, keepdims=True) + EPSILON)
        normed = linear * inv
        win_ref[0, i] = window
        norm_ref[0, i] = normed
        inv_ref[0, i] = inv
        mixed_ref[rows, :] = (normed + window).T.astype(BF16)


def backward_kernel(
    q_ref, k_ref, v_ref, ke_ref, ve_ref, g_ref,
    probs_ref, win_ref, norm_ref, inv_ref, state_ref,
    dq_ref, dk_ref, dv_ref, dke_ref, dve_ref, back_ref,
    kw, vw, dkw, dvw,
):
    tiles = q_ref.shape[0] // TILE
    widen(kw, ke_ref, k_ref)
    widen(vw, ve_ref, v_ref)
    kt = kw[...].T
    causal = causal_t()
    dkw[...] = jnp.zeros_like(dkw)
    dvw[...] = jnp.zeros_like(dvw)
    back = jnp.zeros((DH, DH), F32)
    for i in reversed(range(tiles)):
        rows = slice(i * TILE, (i + 1) * TILE)
        span = slice(i * TILE, i * TILE + SPAN)
        own = slice(LEAD + i * TILE, LEAD + (i + 1) * TILE)
        q, k, v, g = q_ref[rows, :], k_ref[rows, :], v_ref[rows, :], g_ref[rows, :]
        gt = g.astype(F32).T
        normed = norm_ref[0, i]
        delta = jnp.sum(gt * win_ref[0, i], axis=0, keepdims=True)
        inner = jnp.mean(gt * normed, axis=0, keepdims=True)
        gl_f = inv_ref[0, i] * (gt - normed * inner)
        glt = gl_f.astype(BF16)
        gl = gl_f.T.astype(BF16)
        probs = probs_ref[0, i]
        dprob = mm_nt(vw[span, :], g)
        dscore = probs.astype(F32) * ((dprob - delta) * SCALE)
        intra_grad = jnp.where(causal, mm(v, glt), 0.0)
        ds = jnp.concatenate(
            [dscore[:LEAD].astype(BF16), (dscore[LEAD:] + intra_grad).astype(BF16)], axis=0
        )
        intra = jnp.where(causal, mm_nt(k, q), 0.0).astype(BF16)
        rounded = back.astype(BF16)
        dq_ref[rows, :] = (mm(kt[:, span], ds).T + mm(gl, state_ref[0, i])).astype(BF16)
        dkw[span, :] += mm(ds, q)
        dvw[span, :] += mm(probs, g)
        dkw[own, :] += mm(v, rounded)
        dvw[own, :] += mm_nt(k, rounded) + mm(intra, gl)
        back = back + mm(glt, q)
    back_ref[0] = back
    dk_ref[...] = dkw[LEAD:, :]
    dv_ref[...] = dvw[LEAD:, :]
    dke_ref[...] = dkw[LEAD - EDGE : LEAD, :].astype(BF16)
    dve_ref[...] = dvw[LEAD - EDGE : LEAD, :].astype(BF16)


def finish_kernel(k_ref, v_ref, dk_ref, dv_ref, rk_ref, rv_ref, later_ref, gk_ref, gv_ref):
    later = later_ref[0].astype(BF16)
    head = k_ref.shape[0] - EDGE
    dk = dk_ref[...] + mm(v_ref[...], later)
    dv = dv_ref[...] + mm_nt(k_ref[...], later)
    gk_ref[:head, :] = dk[:head].astype(BF16)
    gv_ref[:head, :] = dv[:head].astype(BF16)
    gk_ref[head:, :] = (dk[head:] + rk_ref[...].astype(F32)).astype(BF16)
    gv_ref[head:, :] = (dv[head:] + rv_ref[...].astype(F32)).astype(BF16)


def shifted(shard, by):
    count = lax.axis_size("seq")
    pairs = [(i, i + by) for i in range(count) if 0 <= i + by < count]
    return lax.ppermute(shard, "seq", pairs)


def entering(local, backward):
    count = lax.axis_size("seq")
    place = lax.axis_index("seq")
    gathered = lax.all_gather(local.astype(BF16), "seq")
    order = jnp.arange(count)
    use = order > place if backward else order < place
    return jnp.sum(
        jnp.where(use[:, None, None, None], gathered.astype(F32), 0.0), axis=0
    )


def shards(queries, keys, values, w_out, grad_y):
    tok, width = queries.shape
    groups = width // DH
    tiles = tok // TILE
    place = lax.axis_index("seq")
    tokens_all = tok * lax.axis_size("seq")
    params = pltpu.CompilerParams(
        dimension_semantics=("arbitrary",), vmem_limit_bytes=40 * 1024 * 1024
    )

    def cols(rows):
        return pl.BlockSpec((rows, DH), lambda h: (0, h))

    def heads(*dims):
        return pl.BlockSpec((1,) + dims, lambda h: (h,) + (0,) * len(dims))

    def shape(dims, dtype):
        return jax.ShapeDtypeStruct(dims, dtype)

    def cost(flops, nbytes):
        return pl.CostEstimate(flops=flops, bytes_accessed=nbytes, transcendentals=0)

    ke = shifted(keys[tok - EDGE :], 1)
    ve = shifted(values[tok - EDGE :], 1)
    by_head_k = keys.reshape(tok, groups, DH)
    by_head_v = values.reshape(tok, groups, DH)
    totals = jnp.einsum("thv,thk->hvk", by_head_v, by_head_k, preferred_element_type=F32)
    before = entering(totals, False)
    first = (place * tok).astype(jnp.int32).reshape(1)
    wide = tok + LEAD
    saved = [
        shape((groups, tiles, SPAN, TILE), BF16),
        shape((groups, tiles, DH, TILE), F32),
        shape((groups, tiles, DH, TILE), F32),
        shape((groups, tiles, 1, TILE), F32),
        shape((groups, tiles, DH, DH), BF16),
    ]
    saved_specs = [
        heads(tiles, SPAN, TILE),
        heads(tiles, DH, TILE),
        heads(tiles, DH, TILE),
        heads(tiles, 1, TILE),
        heads(tiles, DH, DH),
    ]
    mixed, *kept = pl.pallas_call(
        forward_kernel,
        grid=(groups,),
        in_specs=[pl.BlockSpec(memory_space=pltpu.SMEM)]
        + [cols(tok)] * 3
        + [cols(EDGE)] * 2
        + [heads(DH, DH)],
        out_specs=[cols(tok)] + saved_specs,
        out_shape=[shape((tok, width), BF16)] + saved,
        scratch_shapes=[pltpu.VMEM((wide, DH), BF16)] * 2,
        compiler_params=params,
        cost_estimate=cost(8 * groups * tok * SPAN * DH, 20 * tok * width),
        name="mixer_forward",
    )(first, queries, keys, values, ke, ve, before)

    grad_full = lax.all_gather(grad_y, "head", axis=1, tiled=True)
    weight = lax.all_gather(w_out, "seq", axis=1, tiled=True)
    weight_part = lax.psum_scatter(
        lax.dot_general(
            grad_full, mixed, (((0,), (0,)), ((), ())), preferred_element_type=F32
        ).astype(BF16),
        "seq",
        scatter_dimension=0,
        tiled=True,
    ).astype(F32)
    projection_sensitivity = weight_part.T * tokens_all ** (-0.5)
    grad_mixed = mm_nt(grad_full, weight).astype(BF16)
    mixer_result = lax.psum_scatter(
        mm(mixed, weight).astype(BF16), "head", scatter_dimension=1, tiled=True
    )

    dq, dk, dv, dke, dve, back = pl.pallas_call(
        backward_kernel,
        grid=(groups,),
        in_specs=[cols(tok)] * 3 + [cols(EDGE)] * 2 + [cols(tok)] + saved_specs,
        out_specs=[cols(tok)] * 3 + [cols(EDGE)] * 2 + [heads(DH, DH)],
        out_shape=[
            shape((tok, width), BF16),
            shape((tok, width), F32),
            shape((tok, width), F32),
            shape((EDGE, width), BF16),
            shape((EDGE, width), BF16),
            shape((groups, DH, DH), F32),
        ],
        scratch_shapes=[pltpu.VMEM((wide, DH), BF16)] * 2 + [pltpu.VMEM((wide, DH), F32)] * 2,
        compiler_params=params,
        cost_estimate=cost(12 * groups * tok * SPAN * DH, 40 * tok * width),
        name="mixer_backward",
    )(queries, keys, values, ke, ve, grad_mixed, *kept)
    rk = shifted(dke, -1)
    rv = shifted(dve, -1)
    later = entering(back, True)
    gk, gv = pl.pallas_call(
        finish_kernel,
        grid=(groups,),
        in_specs=[cols(tok)] * 4 + [cols(EDGE)] * 2 + [heads(DH, DH)],
        out_specs=[cols(tok)] * 2,
        out_shape=[shape((tok, width), BF16)] * 2,
        compiler_params=params,
        cost_estimate=cost(4 * tok * width * DH, 20 * tok * width),
        name="mixer_finish",
    )(keys, values, dk, dv, rk, rv, later)
    return (mixer_result, dq, gk, gv, projection_sensitivity)


def solution(mesh):
    placed = (
        P("seq", "head"),
        P("seq", "head"),
        P("seq", "head"),
        P("head", "seq"),
        P("seq", "head"),
    )
    return jax.shard_map(
        shards,
        mesh=mesh,
        in_specs=placed,
        out_specs=(
            P("seq", "head"),
            P("seq", "head"),
            P("seq", "head"),
            P("seq", "head"),
            P("head", "seq"),
        ),
        check_vma=False,
    )
```

time: 564 us -> 553 us (0.980); the launches traced: 554 us -> 552 us
  waiting for transfers between devices: 332 us -> 424 us
  other arithmetic: 65.1 us -> 7.84 us
  matrix products: 81.1 us -> 31.3 us
  Pallas kernels: 0 us -> 45 us
  local copies, waits for them, and re-layouts: 51.3 us -> 17 us
    all_gather x3, waiting for transfers between devices: 119 us -> 220 us  [the longest x1 127 us: shards(): weight = lax.all_gather(w_out, 'seq', axis=1, tiled=True)]
    ppermute x2 -> x4, waiting for transfers between devices: 72.4 us -> 12.7 us  [shifted(): return lax.ppermute(shard, 'seq', pairs)]
    dot_general x21 -> x4, matrix products: 81.1 us -> 31.3 us  [the longest x1 10.3 us: shards(): lax.dot_general(grad_full, mixed, (((0,), (0,)), ((), ())), preferred_ele...]
    pallas_call x0 -> x3, Pallas kernels: none -> 45 us  [the longest x1 20.5 us: shards(): pl.pallas_call(forward_kernel, grid=(groups,), in_specs=[pl.BlockSpec(mem...]
    reduce_scatter x2, waiting for transfers between devices: 140 us -> 178 us  [the longest x1 134 us: shards(): lax.psum_scatter(lax.dot_general(grad_full, mixed, (((0,), (0,)), ((), ()...]
    sub x2 -> x0, other arithmetic: 20.5 us -> none  [the longest x1 20.5 us: window_block(): raised = jnp.exp(score - row_max[:, None, :])]
    convert_element_type x6 -> x1, other arithmetic: 15.5 us -> 0.76 us  [entering(): gathered = lax.all_gather(local.astype(BF16), 'seq')]
    all_gather x1, waiting for transfers between devices: 0.01 us -> 12.3 us  [shards(): grad_full = lax.all_gather(grad_y, 'head', axis=1, tiled=True)]
  transfers between devices with their start and end apart: 8 -> 10, of which waited for: 5 -> 7; matrix products, arithmetic and copies ran while one was open for 28% -> 5% of each run, Pallas kernels for 0% -> 5%
where the time goes in v1:
time: 553 us; the launch traced here: 552 us
  waiting for transfers between devices  424 us (77%)
  Pallas kernels  45 us (8%)
  matrix products  31.3 us (6%)
  local copies, waits for them, and re-layouts  17 us (3%)
  between operations  14.3 us (3%)
  starting transfers between devices  12.2 us (2%)
  other arithmetic  7.84 us (1%)
    reduce_scatter x1, waiting for transfers between devices, shards(): lax.psum_scatter(lax.dot_general(grad_full, mixed, (((0,), (0,)), ((), ()...  134 us
    all_gather x1, waiting for transfers between devices, shards(): weight = lax.all_gather(w_out, 'seq', axis=1, tiled=True)  127 us
    all_gather x2, waiting for transfers between devices, entering(): gathered = lax.all_gather(local.astype(BF16), 'seq')  92.8 us
    reduce_scatter x1, waiting for transfers between devices, shards(): lax.psum_scatter(mm(mixed, weight).astype(BF16), 'head', scatter_dimensio...  43.8 us
    pallas_call x1, Pallas kernels, shards(): pl.pallas_call(forward_kernel, grid=(groups,), in_specs=[pl.BlockSpec(mem...  20.5 us
    pallas_call x1, Pallas kernels, shards(): pl.pallas_call(backward_kernel, grid=(groups,), in_specs=[cols(tok)] * 3...  17.9 us
    unnamed x30, local copies, waits for them, and re-layouts  13.4 us
    ppermute x4, waiting for transfers between devices, shifted(): return lax.ppermute(shard, 'seq', pairs)  12.7 us
  transfers between devices with their start and end apart: 10, of which 7 were waited for; matrix products, arithmetic and copies ran while one was open for 5% of the time, Pallas kernels for 5%

profile of v1, /device:TPU:0, one launch (start us, length us, event | category | flops | bytes accessed | tf_op | source)
XLA Modules:
  0.0 552.1 jit_solution(16683081420556888468)
XLA Ops:
  7.2 1.6 copy.14
  8.9 2.4 convolution_convert_fusion.2
  13.8 5.8 %collective-permute-start = (bf16[448,1024]{1,0:T(8,128)(2,1)}, bf16[448,1024]{1,0:T(8,128)(2,1)}, u32[]{:S(2)}, u32[]{:S(2)}) collective-permute-start(bf16[448,1024]{1,0:T(8,128)(2,1)} %slice.6), channel_id=1, source_target_pairs={{0,4},{4,8},{8,12},{12,16},{16,20},{20,24},{24,28},{1,5},{5,9},{9,... | collective-permute-start | bytes 2752520 | tf_op jit(solution)/shard_map/ppermute | solution.py:149
  20.6 3.4 collective-permute-start.1
  24.0 55.1 %all-gather.11.cloned.1.call-done = bf16[64,128,128]{2,1,0:T(8,128)(2,1)} async-done(((bf16[8,128,128]{2,1,0:T(8,128)(2,1)}), bf16[64,128,128]{2,1,0:T(8,128)(2,1)}) %all-gather.11.cloned.1.call-update) | async-done | bytes 2097168 | tf_op jit(solution)/shard_map/all_gather | solution.py:155
  79.1 2.1 fusion.1.before_ref
  81.3 20.5 %mixer_forward.1 = (bf16[512,1024]{1,0:T(8,128)(2,1)S(1)}, bf16[8,4,640,128]{3,2,1,0:T(8,128)(2,1)}, f32[8,4,128,128]{3,2,1,0:T(8,128)S(1)}, f32[8,4,128,128]{3,...) custom-call(s32[1]{0:T(128)} %bitcast.first_ref, bf16[512,1024]{1,0:T(8,128)(2,1)S(1)} %copy-done.8, ...), custom_call_target="tpu_custom_call" | custom-call | flops 2684354560 | bytes 10485760 | tf_op jit(solution)/shard_map/mixer_forward/pallas_call | solution.py:207
  103.1 1.3 copy-done.3
  106.4 12.3 %all-gather.9.cloned.1.call-done = bf16[512,4096]{1,0:T(8,128)(2,1)} async-done(((bf16[512,1024]{1,0:T(8,128)(2,1)}), bf16[512,4096]{1,0:T(8,128)(2,1)}) %all-gather.9.cloned.1.call-update) | async-done | bytes 4194320 | tf_op jit(solution)/shard_map/all_gather | solution.py:222
  118.7 127.5 %all-gather.7.cloned.1.call-done = bf16[1024,4096]{1,0:T(8,128)(2,1)} async-done(((bf16[1024,512]{1,0:T(8,128)(2,1)}), bf16[1024,4096]{1,0:T(8,128)(2,1)}) %all-gather.7.cloned.1.call-update) | async-done | bytes 8388624 | tf_op jit(solution)/shard_map/all_gather | solution.py:223
  246.1 9.2 %convolution_convert_fusion.1.g_ref = bf16[512,1024]{1,0:T(8,128)(2,1)S(1)} fusion(bf16[512,4096]{1,0:T(8,128)(2,1)} %all-gather.9.cloned.1.call-done, bf16[1024,4096]{1,0:T(8,128)(2,1)} %all-gather.7.cloned.1.call-done), kind=kOutput, calls=%fused_computation.7 | convolution fusion | flops 4295491584 | bytes 13631488 | tf_op jit(solution)/shard_map/dot_general | solution.py:30
  255.4 17.9 %mixer_backward.1 = (bf16[512,1024]{1,0:T(8,128)(2,1)}, f32[512,1024]{1,0:T(8,128)S(1)}, f32[512,1024]{1,0:T(8,128)S(1)}, bf16[448,1024]{1,0:T(8,128)(2,1)S(1)},...) custom-call(bf16[512,1024]{1,0:T(8,128)(2,1)S(1)} %copy-done.8, bf16[512,1024]{1,0:T(8,128)(2,1)S(1)} %copy-done.1, ...), custom_call_target="tpu_custom_call" | custom-call | flops 4026531840 | bytes 20971520 | tf_op jit(solution)/shard_map/mixer_backward/pallas_call | solution.py:238
  274.6 1.3 copy-done.6
  278.8 10.3 %convert_bitcast_fusion = bf16[4096,1024]{0,1:T(8,128)(2,1)} fusion(bf16[512,1024]{1,0:T(8,128)(2,1)} %copy-done.13, bf16[512,4096]{1,0:T(8,128)(2,1)} %all-gather.9.cloned.1.call-done), kind=kOutput, calls=%fused_computation | convolution fusion | flops 4299161600 | bytes 13631488 | tf_op jit(solution)/shard_map/dot_general | solution.py:225
  290.4 9.4 %convolution_convert_fusion = bf16[512,4096]{1,0:T(8,128)(2,1)} fusion(bf16[512,1024]{1,0:T(8,128)(2,1)S(1)} %copy-done.14, bf16[1024,4096]{1,0:T(8,128)(2,1)} %all-gather.7.cloned.1.call-done), kind=kOutput, calls=%fused_computation.1 | convolution fusion | flops 4297064448 | bytes 13631488 | tf_op jit(solution)/shard_map/dot_general | solution.py:26
  302.4 37.8 %all-gather.13.cloned.1.call-done = bf16[64,128,128]{2,1,0:T(8,128)(2,1)} async-done(((bf16[8,128,128]{2,1,0:T(8,128)(2,1)}), bf16[64,128,128]{2,1,0:T(8,128)(2,1)}) %all-gather.13.cloned.1.call-update) | async-done | bytes 2097168 | tf_op jit(solution)/shard_map/all_gather | solution.py:155
  340.2 2.1 fusion.later_ref
  342.3 12.7 %collective-permute-done.3.rv_ref = bf16[448,1024]{1,0:T(8,128)(2,1)} collective-permute-done((bf16[448,1024]{1,0:T(8,128)(2,1)}, bf16[448,1024]{1,0:T(8,128)(2,1)}, u32[]{:S(2)}, u32[]{:S(2)}) %collective-permute-start.3) | collective-permute-done | bytes 917536 | tf_op jit(solution)/shard_map/ppermute | solution.py:149
  355.0 1.6 copy-done.5
  356.6 1.6 copy-done.7
  358.2 6.6 %mixer_finish.1 = (bf16[512,1024]{1,0:T(8,128)(2,1)}, bf16[512,1024]{1,0:T(8,128)(2,1)}) custom-call(bf16[512,1024]{1,0:T(8,128)(2,1)S(1)} %copy-done.1, bf16[512,1024]{1,0:T(8,128)(2,1)S(1)} %copy-done, f32[512,1024]{1,0:T(8,128)S(1)} %copy-done.5, f32[512,1024]{1,0:T(8,128)S(1)} %copy-done.7, bf16[448,1024]{1,0:T(8,128)(2,1)S(1)} %collective-permute-done.2.rk_ref, ...), custom_call_target="tpu_custom_call" | custom-call | flops 268435456 | bytes 10485760 | tf_op jit(solution)/shard_map/mixer_finish/pallas_call | solution.py:259
  364.9 133.8 %reduce-scatter.5.cloned.1.call-done = bf16[512,1024]{0,1:T(8,128)(2,1)} async-done(((bf16[4096,1024]{0,1:T(8,128)(2,1)}), bf16[512,1024]{0,1:T(8,128)(2,1)}) %reduce-scatter.5.cloned.1.call-update) | async-done | bytes 1048592 | tf_op jit(solution)/shard_map/reduce_scatter | solution.py:224
  498.6 2.8 multiply_bitcast_fusion
  501.5 43.8 %reduce-scatter.3.cloned.1.call-done = bf16[512,1024]{1,0:T(8,128)(2,1)} async-done(((bf16[512,4096]{1,0:T(8,128)(2,1)}), bf16[512,1024]{1,0:T(8,128)(2,1)}) %reduce-scatter.3.cloned.1.call-update) | async-done | bytes 1048592 | tf_op jit(solution)/shard_map/reduce_scatter | solution.py:234
  (48 shorter events, 14.8 us)
Async XLA Ops:
  7.2 5.7 %copy-start.1 = (bf16[512,1024]{1,0:T(8,128)(2,1)S(1)}, bf16[512,1024]{1,0:T(8,128)(2,1)}, u32[]{:S(2)}) copy-start(bf16[512,1024]{1,0:T(8,128)(2,1)} %k_ref.5) | copy-start | bytes 3145732
  7.2 12.5 %copy-start = (bf16[512,1024]{1,0:T(8,128)(2,1)S(1)}, bf16[512,1024]{1,0:T(8,128)(2,1)}, u32[]{:S(2)}) copy-start(bf16[512,1024]{1,0:T(8,128)(2,1)} %v_ref.5) | copy-start | bytes 3145732
  7.2 71.9 %all-gather.11.cloned.1.call-start = ((), (), s32[]{:S(2)}) async-start(), calls=%async_computation.6 | async-start | bytes 2359296 | tf_op jit(solution)/shard_map/all_gather | solution.py:155
  11.3 70.0 %copy-start.8 = (bf16[512,1024]{1,0:T(8,128)(2,1)S(1)}, bf16[512,1024]{1,0:T(8,128)(2,1)}, u32[]{:S(2)}) copy-start(bf16[512,1024]{1,0:T(8,128)(2,1)} %q_ref.3) | copy-start | bytes 3145732
  11.3 107.4 %all-gather.9.cloned.1.call-start = ((), (), s32[]{:S(2)}) async-start(), calls=%async_computation.4 | async-start | bytes 5242880 | tf_op jit(solution)/shard_map/all_gather | solution.py:222
  12.1 234.1 %all-gather.7.cloned.1.call-start = ((), (), s32[]{:S(2)}) async-start(), calls=%async_computation.2 | async-start | bytes 9437184 | tf_op jit(solution)/shard_map/all_gather | solution.py:223
  12.8 327.4 %all-gather.13.cloned.1.call-start = ((), (), s32[]{:S(2)}) async-start(), calls=%async_computation.7 | async-start | bytes 2359296 | tf_op jit(solution)/shard_map/all_gather | solution.py:155
  13.8 67.4 %collective-permute-start = (bf16[448,1024]{1,0:T(8,128)(2,1)}, bf16[448,1024]{1,0:T(8,128)(2,1)}, u32[]{:S(2)}, u32[]{:S(2)}) collective-permute-start(bf16[448,1024]{1,0:T(8,128)(2,1)} %slice.6), channel_id=1, source_target_pairs={{0,4},{4,8},{8,12},{12,16},{16,20},{20,24},{24,28},{1,5},{5,9},{9,... | collective-permute-start | bytes 2752520 | tf_op jit(solution)/shard_map/ppermute | solution.py:149
  20.6 60.7 %collective-permute-start.1 = (bf16[448,1024]{1,0:T(8,128)(2,1)}, bf16[448,1024]{1,0:T(8,128)(2,1)}, u32[]{:S(2)}, u32[]{:S(2)}) collective-permute-start(bf16[448,1024]{1,0:T(8,128)(2,1)} %slice.7), channel_id=1, source_target_pairs={{0,4},{4,8},{8,12},{12,16},{16,20},{20,24},{24,28},{1,5},{5,9},{9,... | collective-permute-start | bytes 2752520 | tf_op jit(solution)/shard_map/ppermute | solution.py:149
  101.8 1.3 copy-start.2
  103.1 1.3 copy-start.3
  104.4 1.0 copy-start.9
  105.4 1.0 copy-start.13
  246.1 9.3 %copy-start.10 = (bf16[8,4,128,128]{3,2,1,0:T(8,128)(2,1)S(1)}, bf16[8,4,128,128]{3,2,1,0:T(8,128)(2,1)}, u32[]{:S(2)}) copy-start(bf16[8,4,128,128]{3,2,1,0:T(8,128)(2,1)} %copy-done.9) | copy-start | bytes 3145732
  273.3 1.3 copy-start.4
  274.6 1.3 copy-start.6
  276.0 0.9 copy-start.11
  278.6 220.0 %reduce-scatter.5.cloned.1.call-start = ((), (), s32[]{:S(2)}) async-start(), calls=%async_computation.5 | async-start | bytes 9437184 | tf_op jit(solution)/shard_map/reduce_scatter | solution.py:224
  289.1 1.2 copy-start.14
  289.2 256.1 %reduce-scatter.3.cloned.1.call-start = ((), (), s32[]{:S(2)}) async-start(), calls=%async_computation.3 | async-start | bytes 5242880 | tf_op jit(solution)/shard_map/reduce_scatter | solution.py:234
  299.8 42.5 %collective-permute-start.2 = (bf16[448,1024]{1,0:T(8,128)(2,1)}, bf16[448,1024]{1,0:T(8,128)(2,1)S(1)}, u32[]{:S(2)}, u32[]{:S(2)}) collective-permute-start(bf16[448,1024]{1,0:T(8,128)(2,1)} %copy-done.12), channel_id=1, source_target_pairs={{4,0},{8,4},{12,8},{16,12},{20,16},{24,20},{28,24},{5,1},{9,5},{13... | collective-permute-start | bytes 2752520 | tf_op jit(solution)/shard_map/ppermute | solution.py:149
  301.1 53.9 %collective-permute-start.3 = (bf16[448,1024]{1,0:T(8,128)(2,1)}, bf16[448,1024]{1,0:T(8,128)(2,1)}, u32[]{:S(2)}, u32[]{:S(2)}) collective-permute-start(bf16[448,1024]{1,0:T(8,128)(2,1)} %copy-done.11), channel_id=1, source_target_pairs={{4,0},{8,4},{12,8},{16,12},{20,16},{24,20},{28,24},{5,1},{9,5},{13... | collective-permute-start | bytes 2752520 | tf_op jit(solution)/shard_map/ppermute | solution.py:149
  355.0 1.6 copy-start.5
  356.6 1.6 copy-start.7
  (1 other events, 0.9 us)
Sparse Core Ops, SparseCore 0:
  11.4 67.6 all-gather.10
  80.7 37.9 all-gather.8
  120.7 125.3 all-gather.6
  278.7 61.3 all-gather.12
  343.6 154.9 reduce-scatter.4
  501.8 43.4 reduce-scatter.2

commit v2 on v1

--- a/solution.py
+++ b/solution.py
@@ -151,13 +151,71 @@
 
 def entering(local, backward):
     count = lax.axis_size("seq")
-    place = lax.axis_index("seq")
-    gathered = lax.all_gather(local.astype(BF16), "seq")
-    order = jnp.arange(count)
-    use = order > place if backward else order < place
-    return jnp.sum(
-        jnp.where(use[:, None, None, None], gathered.astype(F32), 0.0), axis=0
-    )
+    inclusive = local
+    exclusive = jnp.zeros_like(local)
+    step = 1
+    while step < count:
+        arrived = shifted(inclusive.astype(BF16), -step if backward else step).astype(F32)
+        exclusive = exclusive + arrived
+        inclusive = inclusive + arrived
+        step *= 2
+    return exclusive
+
+
+def ring_order(count):
+    return list(range(0, count, 2)) + list(range(count - 1, 0, -2))
+
+
+def ring_place(index, count):
+    return jnp.where(index % 2 == 0, index // 2, count - 1 - index // 2)
+
+
+def ring_owner(place, count):
+    place = lax.rem(place + 2 * count, count)
+    return jnp.where(place < count // 2, 2 * place, 2 * (count - 1 - place) + 1)
+
+
+def ring_step(block, way):
+    count = lax.axis_size("seq")
+    ring = ring_order(count)
+    pairs = [(ring[i], ring[(i + way) % count]) for i in range(count)]
+    return lax.ppermute(block, "seq", pairs)
+
+
+def ring_gather(block):
+    count = lax.axis_size("seq")
+    index = lax.axis_index("seq")
+    place = ring_place(index, count)
+    rows, cols = block.shape
+    half = rows // 2
+    whole = jnp.zeros((rows, cols * count), block.dtype)
+    whole = lax.dynamic_update_slice(whole, block, (0, index * cols))
+    up, down = block[:half], block[half:]
+    for t in range(1, count):
+        up = ring_step(up, 1)
+        down = ring_step(down, -1)
+        whole = lax.dynamic_update_slice(whole, up, (0, ring_owner(place - t, count) * cols))
+        whole = lax.dynamic_update_slice(whole, down, (half, ring_owner(place + t, count) * cols))
+    return whole
+
+
+def ring_scatter(parts):
+    count = lax.axis_size("seq")
+    place = ring_place(lax.axis_index("seq"), count)
+    rows = parts.shape[0] // count
+    half = rows // 2
+
+    def piece(at, lower):
+        start = ring_owner(at, count) * rows + lower * half
+        return lax.dynamic_slice_in_dim(parts, start, half, 0)
+
+    up, down = piece(place - 1, 0), piece(place + 1, 1)
+    for t in range(count - 1):
+        up = ring_step(up, 1).astype(F32) + piece(place - 2 - t, 0).astype(F32)
+        down = ring_step(down, -1).astype(F32) + piece(place + 2 + t, 1).astype(F32)
+        if t < count - 2:
+            up, down = up.astype(BF16), down.astype(BF16)
+    return jnp.concatenate([up, down], axis=0)
 
 
 def shards(queries, keys, values, w_out, grad_y):
@@ -220,15 +278,12 @@
     )(first, queries, keys, values, ke, ve, before)
 
     grad_full = lax.all_gather(grad_y, "head", axis=1, tiled=True)
-    weight = lax.all_gather(w_out, "seq", axis=1, tiled=True)
-    weight_part = lax.psum_scatter(
+    weight = ring_gather(w_out)
+    weight_part = ring_scatter(
         lax.dot_general(
             grad_full, mixed, (((0,), (0,)), ((), ())), preferred_element_type=F32
-        ).astype(BF16),
-        "seq",
-        scatter_dimension=0,
-        tiled=True,
-    ).astype(F32)
+        ).astype(BF16)
+    )
     projection_sensitivity = weight_part.T * tokens_all ** (-0.5)
     grad_mixed = mm_nt(grad_full, weight).astype(BF16)
     mixer_result = lax.psum_scatter(

time: 553 us -> 389 us (0.70)
  waiting for transfers between devices: 424 us -> 147 us
  starting transfers between devices: 12.2 us -> 78.8 us
  local copies, waits for them, and re-layouts: 17 us -> 46.2 us
  other arithmetic: 7.84 us -> 25.2 us
    all_gather x3 -> x0, waiting for transfers between devices: 220 us -> none  [the longest x1 127 us: shards(): weight = lax.all_gather(w_out, 'seq', axis=1, tiled=True)]
    reduce_scatter x1 -> x0, waiting for transfers between devices: 134 us -> none  [shards(): lax.psum_scatter(lax.dot_general(grad_full, mixed, (((0,), (0,)), ((), ()...]
    ppermute x0 -> x28, waiting for transfers between devices: none -> 102 us  [ring_step(): return lax.ppermute(block, 'seq', pairs)]
    ppermute x0 -> x28, starting transfers between devices: none -> 52.2 us  [ring_step(): return lax.ppermute(block, 'seq', pairs)]
    reduce_scatter x1, waiting for transfers between devices: 43.8 us -> 0.01 us  [shards(): lax.psum_scatter(mm(mixed, weight).astype(BF16), 'head', scatter_dimensio...]
    ppermute x4 -> x10, waiting for transfers between devices: 12.7 us -> 44.7 us  [shifted(): return lax.ppermute(shard, 'seq', pairs)]
    dynamic_update_slice x0 -> x15, local copies, waits for them, and re-layouts: none -> 22 us  [the longest x7 10.6 us: ring_gather(): lax.dynamic_update_slice(whole, up, (0, ring_owner(place - t, count) * co...]
    convert_element_type x1 -> x11, other arithmetic: 0.76 us -> 19.6 us  [the longest x6 14.3 us: ring_scatter(): up, down = (up.astype(BF16), down.astype(BF16))]
  transfers between devices with their start and end apart: 10 -> 40, of which waited for: 7 -> 18; matrix products, arithmetic and copies ran while one was open for 5% -> 23% of each run, Pallas kernels for 5% -> 12%
where the time goes in v2:
time: 389 us; the launch traced here: 387 us
  waiting for transfers between devices  147 us (38%)
  starting transfers between devices  78.8 us (20%)
  local copies, waits for them, and re-layouts  46.2 us (12%)
  Pallas kernels  45 us (12%)
  matrix products  30.8 us (8%)
  other arithmetic  25.2 us (6%)
  between operations  14.3 us (4%)
    ppermute x28, waiting for transfers between devices, ring_step(): return lax.ppermute(block, 'seq', pairs)  102 us
    ppermute x28, starting transfers between devices, ring_step(): return lax.ppermute(block, 'seq', pairs)  52.2 us
    ppermute x10, waiting for transfers between devices, shifted(): return lax.ppermute(shard, 'seq', pairs)  44.7 us
    ppermute x10, starting transfers between devices, shifted(): return lax.ppermute(shard, 'seq', pairs)  26.5 us
    pallas_call x1, Pallas kernels, shards(): pl.pallas_call(forward_kernel, grid=(groups,), in_specs=[pl.BlockSpec(mem...  20.5 us
    pallas_call x1, Pallas kernels, shards(): pl.pallas_call(backward_kernel, grid=(groups,), in_specs=[cols(tok)] * 3...  17.8 us
    convert_element_type x6, other arithmetic, ring_scatter(): up, down = (up.astype(BF16), down.astype(BF16))  14.3 us
    unnamed x38, local copies, waits for them, and re-layouts  12.8 us
  transfers between devices with their start and end apart: 40, of which 18 were waited for; matrix products, arithmetic and copies ran while one was open for 23% of the time, Pallas kernels for 12%

profile of v2, /device:TPU:0, one launch (start us, length us, event | category | flops | bytes accessed | tf_op | source)
XLA Modules:
  0.0 387.2 jit_solution(5446643131725550374)
XLA Ops:
  12.3 12.0 %collective-permute-done.5 = bf16[512,512]{1,0:T(8,128)(2,1)} collective-permute-done((bf16[512,512]{1,0:T(8,128)(2,1)S(1)}, bf16[512,512]{1,0:T(8,128)(2,1)}, u32[]{:S(2)}, u32[]{:S(2)}) %collective-permute-start.5) | collective-permute-done | bytes 524320 | tf_op jit(solution)/shard_map/ppermute | solution.py:182
  33.2 4.5 %collective-permute-done.7 = bf16[512,512]{1,0:T(8,128)(2,1)} collective-permute-done((bf16[512,512]{1,0:T(8,128)(2,1)}, bf16[512,512]{1,0:T(8,128)(2,1)}, u32[]{:S(2)}, u32[]{:S(2)}) %collective-permute-start.7) | collective-permute-done | bytes 524320 | tf_op jit(solution)/shard_map/ppermute | solution.py:182
  45.3 6.3 %collective-permute-start.3 = (bf16[8,128,128]{2,1,0:T(8,128)(2,1)}, bf16[8,128,128]{2,1,0:T(8,128)(2,1)}, u32[]{:S(2)}, u32[]{:S(2)}) collective-permute-start(bf16[8,128,128]{2,1,0:T(8,128)(2,1)} %fusion.21), channel_id=1, source_target_pairs={{0,8},{4,12},{8,16},{12,20},{16,24},{20,28},{1,9},{5,13},{9,17},{1... | collective-permute-start | bytes 786440 | tf_op jit(solution)/shard_map/ppermute | solution.py:149
  56.2 4.6 %collective-permute-start.1 = (bf16[448,1024]{1,0:T(8,128)(2,1)}, bf16[448,1024]{1,0:T(8,128)(2,1)}, u32[]{:S(2)}, u32[]{:S(2)}) collective-permute-start(bf16[448,1024]{1,0:T(8,128)(2,1)} %slice.13), channel_id=1, source_target_pairs={{0,4},{4,8},{8,12},{12,16},{16,20},{20,24},{24,28},{1,5},{5,9},{9,... | collective-permute-start | bytes 2752520 | tf_op jit(solution)/shard_map/ppermute | solution.py:149
  62.8 4.3 %broadcast_in_dim.3 = bf16[1024,4096]{1,0:T(8,128)(2,1)} broadcast(bf16[]{:T(256)} %constant.160.clone.1), dimensions={} | broadcast | bytes 8388610 | tf_op jit(solution)/shard_map/broadcast_in_dim | solution.py:191
  76.8 27.6 %collective-permute-done.12 = bf16[512,512]{1,0:T(8,128)(2,1)} collective-permute-done((bf16[512,512]{1,0:T(8,128)(2,1)}, bf16[512,512]{1,0:T(8,128)(2,1)}, u32[]{:S(2)}, u32[]{:S(2)}) %collective-permute-start.12) | collective-permute-done | bytes 524320 | tf_op jit(solution)/shard_map/ppermute | solution.py:182
  104.4 9.4 %collective-permute-start.14 = (bf16[512,512]{1,0:T(8,128)(2,1)}, bf16[512,512]{1,0:T(8,128)(2,1)S(1)}, u32[]{:S(2)}, u32[]{:S(2)}) collective-permute-start(bf16[512,512]{1,0:T(8,128)(2,1)} %collective-permute-done.12), channel_id=1, source_target_pairs={{0,4},{8,0},{16,8},{24,16},{28,24},{20,28},{12,20},{4,12},{1,5},{9... | collective-permute-start | bytes 1572872 | tf_op jit(solution)/shard_map/ppermute | solution.py:182
  114.9 20.5 %mixer_forward.1 = (bf16[512,1024]{1,0:T(8,128)(2,1)S(1)}, bf16[8,4,640,128]{3,2,1,0:T(8,128)(2,1)}, f32[8,4,128,128]{3,2,1,0:T(8,128)S(1)}, f32[8,4,128,128]{3,...) custom-call(s32[1]{0:T(128)} %bitcast.first_ref, bf16[512,1024]{1,0:T(8,128)(2,1)S(1)} %copy-done.8, ...), custom_call_target="tpu_custom_call" | custom-call | flops 2684354560 | bytes 10485760 | tf_op jit(solution)/shard_map/mixer_forward/pallas_call | solution.py:265
  141.3 6.8 %collective-permute-start.16 = (bf16[512,512]{1,0:T(8,128)(2,1)S(1)}, bf16[512,512]{1,0:T(8,128)(2,1)S(1)}, u32[]{:S(2)}, u32[]{:S(2)}) collective-permute-start(bf16[512,512]{1,0:T(8,128)(2,1)S(1)} %collective-permute-done.14), channel_id=1, source_target_pairs={{0,4},{8,0},{16,8},{24,16},{28,24},{20,28},{12,20},{4,12},{1,5},{9... | collective-permute-start | bytes 1572872 | tf_op jit(solution)/shard_map/ppermute | solution.py:182
  157.7 6.0 %collective-permute-start.18 = (bf16[512,512]{1,0:T(8,128)(2,1)S(1)}, bf16[512,512]{1,0:T(8,128)(2,1)S(1)}, u32[]{:S(2)}, u32[]{:S(2)}) collective-permute-start(bf16[512,512]{1,0:T(8,128)(2,1)S(1)} %collective-permute-done.16), channel_id=1, source_target_pairs={{0,4},{8,0},{16,8},{24,16},{28,24},{20,28},{12,20},{4,12},{1,5},{9... | collective-permute-start | bytes 1572872 | tf_op jit(solution)/shard_map/ppermute | solution.py:182
  171.3 9.4 %convolution_convert_fusion.1 = bf16[512,4096]{1,0:T(8,128)(2,1)} fusion(bf16[512,1024]{1,0:T(8,128)(2,1)S(1)} %get-tuple-element.19, bf16[1024,4096]{1,0:T(8,128)(2,1)} %constant_dynamic-update-slice_fusion.8), kind=kOutput, calls=%fused_computation.1 | convolution fusion | flops 4297064448 | bytes 13631488 | tf_op jit(solution)/shard_map/dot_general | solution.py:26
  180.8 10.6 %convolution_convert_fusion = bf16[1024,4096]{1,0:T(8,128)(2,1)} fusion(bf16[512,1024]{1,0:T(8,128)(2,1)} %copy-done.14, bf16[512,4096]{1,0:T(8,128)(2,1)} %all-gather.2.cloned.1.call-done), kind=kOutput, calls=%fused_computation | convolution fusion | flops 4299161600 | bytes 13631488 | tf_op jit(solution)/shard_map/dot_general | solution.py:283
  193.8 4.2 %collective-permute-start.24 = (bf16[256,1024]{0,1:T(8,128)(2,1)}, bf16[256,1024]{0,1:T(8,128)(2,1)S(1)}, u32[]{:S(2)}, u32[]{:S(2)}) collective-permute-start(bf16[256,1024]{0,1:T(8,128)(2,1)} %get-tuple-element.47), channel_id=1, source_target_pairs={{0,8},{8,16},{16,24},{24,28},{28,20},{20,12},{12,4},{4,0},{1,9},{9... | collective-permute-start | bytes 1572872 | tf_op jit(solution)/shard_map/ppermute | solution.py:182
  198.0 7.5 %collective-permute-done.24 = bf16[256,1024]{0,1:T(8,128)(2,1)S(1)} collective-permute-done((bf16[256,1024]{0,1:T(8,128)(2,1)}, bf16[256,1024]{0,1:T(8,128)(2,1)S(1)}, u32[]{:S(2)}, u32[]{:S(2)}) %collective-permute-start.24) | collective-permute-done | bytes 524320 | tf_op jit(solution)/shard_map/ppermute | solution.py:182
  213.0 9.0 %collective-permute-done.25 = bf16[256,1024]{0,1:T(8,128)(2,1)S(1)} collective-permute-done((bf16[256,1024]{0,1:T(8,128)(2,1)}, bf16[256,1024]{0,1:T(8,128)(2,1)S(1)}, u32[]{:S(2)}, u32[]{:S(2)}) %collective-permute-start.25) | collective-permute-done | bytes 524320 | tf_op jit(solution)/shard_map/ppermute | solution.py:182
  221.9 5.3 %collective-permute-done.32 = bf16[256,1024]{0,1:T(8,128)(2,1)} collective-permute-done((bf16[256,1024]{0,1:T(8,128)(2,1)S(1)}, bf16[256,1024]{0,1:T(8,128)(2,1)}, u32[]{:S(2)}, u32[]{:S(2)}) %collective-permute-start.32) | collective-permute-done | bytes 524320 | tf_op jit(solution)/shard_map/ppermute | solution.py:182
  232.0 11.8 %collective-permute-done.26 = bf16[256,1024]{0,1:T(8,128)(2,1)S(1)} collective-permute-done((bf16[256,1024]{0,1:T(8,128)(2,1)}, bf16[256,1024]{0,1:T(8,128)(2,1)S(1)}, u32[]{:S(2)}, u32[]{:S(2)}) %collective-permute-start.26) | collective-permute-done | bytes 524320 | tf_op jit(solution)/shard_map/ppermute | solution.py:182
  251.1 11.2 %collective-permute-done.27 = bf16[256,1024]{0,1:T(8,128)(2,1)S(1)} collective-permute-done((bf16[256,1024]{0,1:T(8,128)(2,1)}, bf16[256,1024]{0,1:T(8,128)(2,1)S(1)}, u32[]{:S(2)}, u32[]{:S(2)}) %collective-permute-start.27) | collective-permute-done | bytes 524320 | tf_op jit(solution)/shard_map/ppermute | solution.py:182
  266.4 9.1 %fusion.1.g_ref = bf16[512,1024]{1,0:T(8,128)(2,1)S(1)} fusion(bf16[1024,4096]{1,0:T(8,128)(2,1)} %constant_dynamic-update-slice_fusion.8, bf16[512,4096]{1,0:T(8,128)(2,1)} %all-gather.2.cloned.1.call-done), kind=kOutput, calls=%fused_computation.5 | convolution fusion | flops 4295491584 | bytes 13631488 | tf_op jit(solution)/shard_map/dot_general | solution.py:30
  275.6 17.8 %mixer_backward.1 = (bf16[512,1024]{1,0:T(8,128)(2,1)}, f32[512,1024]{1,0:T(8,128)S(1)}, f32[512,1024]{1,0:T(8,128)S(1)}, bf16[448,1024]{1,0:T(8,128)(2,1)S(1)},...) custom-call(bf16[512,1024]{1,0:T(8,128)(2,1)S(1)} %copy-done.9, bf16[512,1024]{1,0:T(8,128)(2,1)S(1)} %copy-done.1, ...), custom_call_target="tpu_custom_call" | custom-call | flops 4026531840 | bytes 20971520 | tf_op jit(solution)/shard_map/mixer_backward/pallas_call | solution.py:293
  314.4 12.5 %collective-permute-done.22 = bf16[8,128,128]{2,1,0:T(8,128)(2,1)} collective-permute-done((bf16[8,128,128]{2,1,0:T(8,128)(2,1)}, bf16[8,128,128]{2,1,0:T(8,128)(2,1)}, u32[]{:S(2)}, u32[]{:S(2)}) %collective-permute-start.22) | collective-permute-done | bytes 262176 | tf_op jit(solution)/shard_map/ppermute | solution.py:149
  330.0 5.4 %collective-permute-done.36 = bf16[256,1024]{0,1:T(8,128)(2,1)} collective-permute-done((bf16[256,1024]{0,1:T(8,128)(2,1)}, bf16[256,1024]{0,1:T(8,128)(2,1)}, u32[]{:S(2)}, u32[]{:S(2)}) %collective-permute-start.36) | collective-permute-done | bytes 524320 | tf_op jit(solution)/shard_map/ppermute | solution.py:182
  340.8 25.3 %collective-permute-done.23 = bf16[8,128,128]{2,1,0:T(8,128)(2,1)} collective-permute-done((bf16[8,128,128]{2,1,0:T(8,128)(2,1)}, bf16[8,128,128]{2,1,0:T(8,128)(2,1)}, u32[]{:S(2)}, u32[]{:S(2)}) %collective-permute-start.23) | collective-permute-done | bytes 262176 | tf_op jit(solution)/shard_map/ppermute | solution.py:149
  370.5 6.6 %mixer_finish.1 = (bf16[512,1024]{1,0:T(8,128)(2,1)}, bf16[512,1024]{1,0:T(8,128)(2,1)}) custom-call(bf16[512,1024]{1,0:T(8,128)(2,1)S(1)} %copy-done.1, bf16[512,1024]{1,0:T(8,128)(2,1)S(1)} %copy-done, f32[512,1024]{1,0:T(8,128)S(1)} %copy-done.5, f32[512,1024]{1,0:T(8,128)S(1)} %copy-done.7, bf16[448,1024]{1,0:T(8,128)(2,1)S(1)} %collective-permute-done.19.rk_ref, ...), custom_call_target="tpu_custom_call" | custom-call | flops 268435456 | bytes 10485760 | tf_op jit(solution)/shard_map/mixer_finish/pallas_call | solution.py:314
  (139 shorter events, 125.1 us)
Async XLA Ops:
  7.2 173.6 %all-gather.2.cloned.1.call-start = ((), (), s32[]{:S(2)}) async-start(), calls=%async_computation.2 | async-start | bytes 5242880 | tf_op jit(solution)/shard_map/all_gather | solution.py:280
  7.9 372.5 %reduce-scatter.2.cloned.1.call-start = ((), (), s32[]{:S(2)}) async-start(), calls=%async_computation.1 | async-start | bytes 5242880 | tf_op jit(solution)/shard_map/reduce_scatter | solution.py:289
  9.2 15.0 %collective-permute-start.5 = (bf16[512,512]{1,0:T(8,128)(2,1)S(1)}, bf16[512,512]{1,0:T(8,128)(2,1)}, u32[]{:S(2)}, u32[]{:S(2)}) collective-permute-start(bf16[512,512]{1,0:T(8,128)(2,1)S(1)} %get-tuple-element.50), channel_id=1, source_target_pairs={{0,8},{8,16},{16,24},{24,28},{28,20},{20,12},{12,4},{4,0},{1,9},{9... | collective-permute-start | bytes 1572872 | tf_op jit(solution)/shard_map/ppermute | solution.py:182
  37.7 23.1 %collective-permute-start.9 = (bf16[512,512]{1,0:T(8,128)(2,1)}, bf16[512,512]{1,0:T(8,128)(2,1)}, u32[]{:S(2)}, u32[]{:S(2)}) collective-permute-start(bf16[512,512]{1,0:T(8,128)(2,1)} %collective-permute-done.7), channel_id=1, source_target_pairs={{0,8},{8,16},{16,24},{24,28},{28,20},{20,12},{12,4},{4,0},{1,9},{9... | collective-permute-start | bytes 1572872 | tf_op jit(solution)/shard_map/ppermute | solution.py:182
  39.2 22.3 %collective-permute-start.10 = (bf16[512,512]{1,0:T(8,128)(2,1)}, bf16[512,512]{1,0:T(8,128)(2,1)}, u32[]{:S(2)}, u32[]{:S(2)}) collective-permute-start(bf16[512,512]{1,0:T(8,128)(2,1)} %collective-permute-done.8), channel_id=1, source_target_pairs={{0,4},{8,0},{16,8},{24,16},{28,24},{20,28},{12,20},{4,12},{1,5},{9... | collective-permute-start | bytes 1572872 | tf_op jit(solution)/shard_map/ppermute | solution.py:182
  45.3 22.9 %collective-permute-start.3 = (bf16[8,128,128]{2,1,0:T(8,128)(2,1)}, bf16[8,128,128]{2,1,0:T(8,128)(2,1)}, u32[]{:S(2)}, u32[]{:S(2)}) collective-permute-start(bf16[8,128,128]{2,1,0:T(8,128)(2,1)} %fusion.21), channel_id=1, source_target_pairs={{0,8},{4,12},{8,16},{12,20},{16,24},{20,28},{1,9},{5,13},{9,17},{1... | collective-permute-start | bytes 786440 | tf_op jit(solution)/shard_map/ppermute | solution.py:149
  52.5 62.4 %collective-permute-start = (bf16[448,1024]{1,0:T(8,128)(2,1)}, bf16[448,1024]{1,0:T(8,128)(2,1)}, u32[]{:S(2)}, u32[]{:S(2)}) collective-permute-start(bf16[448,1024]{1,0:T(8,128)(2,1)} %slice.12), channel_id=1, source_target_pairs={{0,4},{4,8},{8,12},{12,16},{16,20},{20,24},{24,28},{1,5},{5,9},{9,... | collective-permute-start | bytes 2752520 | tf_op jit(solution)/shard_map/ppermute | solution.py:149
  56.2 58.8 %collective-permute-start.1 = (bf16[448,1024]{1,0:T(8,128)(2,1)}, bf16[448,1024]{1,0:T(8,128)(2,1)}, u32[]{:S(2)}, u32[]{:S(2)}) collective-permute-start(bf16[448,1024]{1,0:T(8,128)(2,1)} %slice.13), channel_id=1, source_target_pairs={{0,4},{4,8},{8,12},{12,16},{16,20},{20,24},{24,28},{1,5},{5,9},{9,... | collective-permute-start | bytes 2752520 | tf_op jit(solution)/shard_map/ppermute | solution.py:149
  61.5 42.9 %collective-permute-start.12 = (bf16[512,512]{1,0:T(8,128)(2,1)}, bf16[512,512]{1,0:T(8,128)(2,1)}, u32[]{:S(2)}, u32[]{:S(2)}) collective-permute-start(bf16[512,512]{1,0:T(8,128)(2,1)} %collective-permute-done.10), channel_id=1, source_target_pairs={{0,4},{8,0},{16,8},{24,16},{28,24},{20,28},{12,20},{4,12},{1,5},{9... | collective-permute-start | bytes 1572872 | tf_op jit(solution)/shard_map/ppermute | solution.py:182
  70.1 43.7 %collective-permute-start.4 = (bf16[8,128,128]{2,1,0:T(8,128)(2,1)}, bf16[8,128,128]{2,1,0:T(8,128)(2,1)}, u32[]{:S(2)}, u32[]{:S(2)}) collective-permute-start(bf16[8,128,128]{2,1,0:T(8,128)(2,1)} %fusion.18), channel_id=1, source_target_pairs={{0,16},{4,20},{8,24},{12,28},{1,17},{5,21},{9,25},{13,29},{2,18},{... | collective-permute-start | bytes 786440 | tf_op jit(solution)/shard_map/ppermute | solution.py:149
  74.9 64.1 %collective-permute-start.13 = (bf16[512,512]{1,0:T(8,128)(2,1)}, bf16[512,512]{1,0:T(8,128)(2,1)S(1)}, u32[]{:S(2)}, u32[]{:S(2)}) collective-permute-start(bf16[512,512]{1,0:T(8,128)(2,1)} %collective-permute-done.11), channel_id=1, source_target_pairs={{0,8},{8,16},{16,24},{24,28},{28,20},{20,12},{12,4},{4,0},{1,9},{9... | collective-permute-start | bytes 1572872 | tf_op jit(solution)/shard_map/ppermute | solution.py:182
  104.4 36.9 %collective-permute-start.14 = (bf16[512,512]{1,0:T(8,128)(2,1)}, bf16[512,512]{1,0:T(8,128)(2,1)S(1)}, u32[]{:S(2)}, u32[]{:S(2)}) collective-permute-start(bf16[512,512]{1,0:T(8,128)(2,1)} %collective-permute-done.12), channel_id=1, source_target_pairs={{0,4},{8,0},{16,8},{24,16},{28,24},{20,28},{12,20},{4,12},{1,5},{9... | collective-permute-start | bytes 1572872 | tf_op jit(solution)/shard_map/ppermute | solution.py:182
  139.0 16.8 %collective-permute-start.15 = (bf16[512,512]{1,0:T(8,128)(2,1)S(1)}, bf16[512,512]{1,0:T(8,128)(2,1)S(1)}, u32[]{:S(2)}, u32[]{:S(2)}) collective-permute-start(bf16[512,512]{1,0:T(8,128)(2,1)S(1)} %collective-permute-done.13), channel_id=1, source_target_pairs={{0,8},{8,16},{16,24},{24,28},{28,20},{20,12},{12,4},{4,0},{1,9},{9... | collective-permute-start | bytes 1572872 | tf_op jit(solution)/shard_map/ppermute | solution.py:182
  141.3 16.4 %collective-permute-start.16 = (bf16[512,512]{1,0:T(8,128)(2,1)S(1)}, bf16[512,512]{1,0:T(8,128)(2,1)S(1)}, u32[]{:S(2)}, u32[]{:S(2)}) collective-permute-start(bf16[512,512]{1,0:T(8,128)(2,1)S(1)} %collective-permute-done.14), channel_id=1, source_target_pairs={{0,4},{8,0},{16,8},{24,16},{28,24},{20,28},{12,20},{4,12},{1,5},{9... | collective-permute-start | bytes 1572872 | tf_op jit(solution)/shard_map/ppermute | solution.py:182
  264.4 34.8 %collective-permute-start.28 = (bf16[256,1024]{0,1:T(8,128)(2,1)S(1)}, bf16[256,1024]{0,1:T(8,128)(2,1)S(1)}, u32[]{:S(2)}, u32[]{:S(2)}) collective-permute-start(bf16[256,1024]{0,1:T(8,128)(2,1)S(1)} %get-tuple-element.39), channel_id=1, source_target_pairs={{0,8},{8,16},{16,24},{24,28},{28,20},{20,12},{12,4},{4,0},{1,9},{9... | collective-permute-start | bytes 1572872 | tf_op jit(solution)/shard_map/ppermute | solution.py:182
  264.5 34.7 %collective-permute-start.35 = (bf16[256,1024]{0,1:T(8,128)(2,1)S(1)}, bf16[256,1024]{0,1:T(8,128)(2,1)S(1)}, u32[]{:S(2)}, u32[]{:S(2)}) collective-permute-start(bf16[256,1024]{0,1:T(8,128)(2,1)S(1)} %get-tuple-element.40), channel_id=1, source_target_pairs={{0,4},{8,0},{16,8},{24,16},{28,24},{20,28},{12,20},{4,12},{1,5},{9... | collective-permute-start | bytes 1572872 | tf_op jit(solution)/shard_map/ppermute | solution.py:182
  301.7 28.4 %collective-permute-start.29 = (bf16[256,1024]{0,1:T(8,128)(2,1)}, bf16[256,1024]{0,1:T(8,128)(2,1)}, u32[]{:S(2)}, u32[]{:S(2)}) collective-permute-start(bf16[256,1024]{0,1:T(8,128)(2,1)} %get-tuple-element.37), channel_id=1, source_target_pairs={{0,8},{8,16},{16,24},{24,28},{28,20},{20,12},{12,4},{4,0},{1,9},{9... | collective-permute-start | bytes 1572872 | tf_op jit(solution)/shard_map/ppermute | solution.py:182
  305.2 30.2 %collective-permute-start.36 = (bf16[256,1024]{0,1:T(8,128)(2,1)}, bf16[256,1024]{0,1:T(8,128)(2,1)}, u32[]{:S(2)}, u32[]{:S(2)}) collective-permute-start(bf16[256,1024]{0,1:T(8,128)(2,1)} %get-tuple-element.38), channel_id=1, source_target_pairs={{0,4},{8,0},{16,8},{24,16},{28,24},{20,28},{12,20},{4,12},{1,5},{9... | collective-permute-start | bytes 1572872 | tf_op jit(solution)/shard_map/ppermute | solution.py:182
  310.5 16.4 %collective-permute-start.22 = (bf16[8,128,128]{2,1,0:T(8,128)(2,1)}, bf16[8,128,128]{2,1,0:T(8,128)(2,1)}, u32[]{:S(2)}, u32[]{:S(2)}) collective-permute-start(bf16[8,128,128]{2,1,0:T(8,128)(2,1)} %fusion.22), channel_id=1, source_target_pairs={{8,0},{12,4},{16,8},{20,12},{24,16},{28,20},{9,1},{13,5},{17,9},{2... | collective-permute-start | bytes 786440 | tf_op jit(solution)/shard_map/ppermute | solution.py:149
  311.8 55.5 %collective-permute-start.19 = (bf16[448,1024]{1,0:T(8,128)(2,1)}, bf16[448,1024]{1,0:T(8,128)(2,1)S(1)}, u32[]{:S(2)}, u32[]{:S(2)}) collective-permute-start(bf16[448,1024]{1,0:T(8,128)(2,1)} %copy-done.13), channel_id=1, source_target_pairs={{4,0},{8,4},{12,8},{16,12},{20,16},{24,20},{28,24},{5,1},{9,5},{13... | collective-permute-start | bytes 2752520 | tf_op jit(solution)/shard_map/ppermute | solution.py:149
  313.1 54.2 %collective-permute-start.20 = (bf16[448,1024]{1,0:T(8,128)(2,1)}, bf16[448,1024]{1,0:T(8,128)(2,1)}, u32[]{:S(2)}, u32[]{:S(2)}) collective-permute-start(bf16[448,1024]{1,0:T(8,128)(2,1)} %copy-done.12), channel_id=1, source_target_pairs={{4,0},{8,4},{12,8},{16,12},{20,16},{24,20},{28,24},{5,1},{9,5},{13... | collective-permute-start | bytes 2752520 | tf_op jit(solution)/shard_map/ppermute | solution.py:149
  328.7 37.4 %collective-permute-start.23 = (bf16[8,128,128]{2,1,0:T(8,128)(2,1)}, bf16[8,128,128]{2,1,0:T(8,128)(2,1)}, u32[]{:S(2)}, u32[]{:S(2)}) collective-permute-start(bf16[8,128,128]{2,1,0:T(8,128)(2,1)} %fusion.20), channel_id=1, source_target_pairs={{16,0},{20,4},{24,8},{28,12},{17,1},{21,5},{25,9},{29,13},{18,2},{... | collective-permute-start | bytes 786440 | tf_op jit(solution)/shard_map/ppermute | solution.py:149
  338.2 39.0 %collective-permute-start.30 = (bf16[256,1024]{0,1:T(8,128)(2,1)}, bf16[256,1024]{0,1:T(8,128)(2,1)S(1)}, u32[]{:S(2)}, u32[]{:S(2)}) collective-permute-start(bf16[256,1024]{0,1:T(8,128)(2,1)} %get-tuple-element.35), channel_id=1, source_target_pairs={{0,8},{8,16},{16,24},{24,28},{28,20},{20,12},{12,4},{4,0},{1,9},{9... | collective-permute-start | bytes 1572872 | tf_op jit(solution)/shard_map/ppermute | solution.py:182
  338.2 39.0 %collective-permute-start.37 = (bf16[256,1024]{0,1:T(8,128)(2,1)}, bf16[256,1024]{0,1:T(8,128)(2,1)}, u32[]{:S(2)}, u32[]{:S(2)}) collective-permute-start(bf16[256,1024]{0,1:T(8,128)(2,1)} %get-tuple-element.36), channel_id=1, source_target_pairs={{0,4},{8,0},{16,8},{24,16},{28,24},{20,28},{12,20},{4,12},{1,5},{9... | collective-permute-start | bytes 1572872 | tf_op jit(solution)/shard_map/ppermute | solution.py:182
  (35 other events, 459.2 us)
Sparse Core Ops, SparseCore 0:
  9.6 37.1 all-gather.1
  180.9 48.0 reduce-scatter.1

commit v3 on v2

--- a/solution.py
+++ b/solution.py
@@ -182,7 +182,7 @@
     return lax.ppermute(block, "seq", pairs)
 
 
-def ring_gather(block):
+def ring_gather(block, after):
     count = lax.axis_size("seq")
     index = lax.axis_index("seq")
     place = ring_place(index, count)
@@ -192,6 +192,8 @@
     whole = lax.dynamic_update_slice(whole, block, (0, index * cols))
     up, down = block[:half], block[half:]
     for t in range(1, count):
+        if 2 <= t < 2 + len(after):
+            up, down, _ = lax.optimization_barrier((up, down, after[t - 2]))
         up = ring_step(up, 1)
         down = ring_step(down, -1)
         whole = lax.dynamic_update_slice(whole, up, (0, ring_owner(place - t, count) * cols))
@@ -199,23 +201,30 @@
     return whole
 
 
-def ring_scatter(parts):
+def ring_scatter(parts, after):
     count = lax.axis_size("seq")
     place = ring_place(lax.axis_index("seq"), count)
     rows = parts.shape[0] // count
-    half = rows // 2
-
-    def piece(at, lower):
-        start = ring_owner(at, count) * rows + lower * half
-        return lax.dynamic_slice_in_dim(parts, start, half, 0)
-
-    up, down = piece(place - 1, 0), piece(place + 1, 1)
+    part = rows // 4
+
+    def piece(at, number):
+        start = ring_owner(at, count) * rows + number * part
+        return lax.dynamic_slice_in_dim(parts, start, part, 0)
+
+    ways = (1, -1, 1, -1)
+    sums = [piece(place - way, number) for number, way in enumerate(ways)]
     for t in range(count - 1):
-        up = ring_step(up, 1).astype(F32) + piece(place - 2 - t, 0).astype(F32)
-        down = ring_step(down, -1).astype(F32) + piece(place + 2 + t, 1).astype(F32)
-        if t < count - 2:
-            up, down = up.astype(BF16), down.astype(BF16)
-    return jnp.concatenate([up, down], axis=0)
+        if t in after:
+            *sums, _ = lax.optimization_barrier((*sums, after[t]))
+        source = parts
+        for number, way in enumerate(ways):
+            arrived = ring_step(sums[number], way).astype(F32)
+            start = ring_owner(place - way * (2 + t), count) * rows + number * part
+            total = arrived + lax.dynamic_slice_in_dim(source, start, part, 0).astype(F32)
+            sums[number] = total.astype(BF16) if t < count - 2 else total
+            if number == 1 and t < count - 2:
+                source, _ = lax.optimization_barrier((parts, sums[0]))
+    return jnp.concatenate(sums, axis=0)
 
 
 def shards(queries, keys, values, w_out, grad_y):
@@ -228,8 +237,8 @@
         dimension_semantics=("arbitrary",), vmem_limit_bytes=40 * 1024 * 1024
     )
 
-    def cols(rows):
-        return pl.BlockSpec((rows, DH), lambda h: (0, h))
+    def cols(rows, skip=0):
+        return pl.BlockSpec((rows, DH), lambda h: (0, h + skip))
 
     def heads(*dims):
         return pl.BlockSpec((1,) + dims, lambda h: (h,) + (0,) * len(dims))
@@ -240,20 +249,22 @@
     def cost(flops, nbytes):
         return pl.CostEstimate(flops=flops, bytes_accessed=nbytes, transcendentals=0)
 
-    ke = shifted(keys[tok - EDGE :], 1)
-    ve = shifted(values[tok - EDGE :], 1)
+    count = 2
+    part = groups // count
+    spans = [slice(c * part * DH, (c + 1) * part * DH) for c in range(count)]
     by_head_k = keys.reshape(tok, groups, DH)
     by_head_v = values.reshape(tok, groups, DH)
     totals = jnp.einsum("thv,thk->hvk", by_head_v, by_head_k, preferred_element_type=F32)
     before = entering(totals, False)
+    halo = [(shifted(keys[tok - EDGE :, c], 1), shifted(values[tok - EDGE :, c], 1)) for c in spans]
     first = (place * tok).astype(jnp.int32).reshape(1)
     wide = tok + LEAD
     saved = [
-        shape((groups, tiles, SPAN, TILE), BF16),
-        shape((groups, tiles, DH, TILE), F32),
-        shape((groups, tiles, DH, TILE), F32),
-        shape((groups, tiles, 1, TILE), F32),
-        shape((groups, tiles, DH, DH), BF16),
+        shape((part, tiles, SPAN, TILE), BF16),
+        shape((part, tiles, DH, TILE), F32),
+        shape((part, tiles, DH, TILE), F32),
+        shape((part, tiles, 1, TILE), F32),
+        shape((part, tiles, DH, DH), BF16),
     ]
     saved_specs = [
         heads(tiles, SPAN, TILE),
@@ -262,65 +273,92 @@
         heads(tiles, 1, TILE),
         heads(tiles, DH, DH),
     ]
-    mixed, *kept = pl.pallas_call(
-        forward_kernel,
-        grid=(groups,),
-        in_specs=[pl.BlockSpec(memory_space=pltpu.SMEM)]
-        + [cols(tok)] * 3
-        + [cols(EDGE)] * 2
-        + [heads(DH, DH)],
-        out_specs=[cols(tok)] + saved_specs,
-        out_shape=[shape((tok, width), BF16)] + saved,
-        scratch_shapes=[pltpu.VMEM((wide, DH), BF16)] * 2,
-        compiler_params=params,
-        cost_estimate=cost(8 * groups * tok * SPAN * DH, 20 * tok * width),
-        name="mixer_forward",
-    )(first, queries, keys, values, ke, ve, before)
-
     grad_full = lax.all_gather(grad_y, "head", axis=1, tiled=True)
-    weight = ring_gather(w_out)
-    weight_part = ring_scatter(
-        lax.dot_general(
-            grad_full, mixed, (((0,), (0,)), ((), ())), preferred_element_type=F32
-        ).astype(BF16)
+    weight = ring_gather(w_out, [halo[0], (halo[1], before)])
+
+    mixed_parts, kept = [], []
+    for c in range(count):
+        skip = c * part
+        mixed_part, *rest = pl.pallas_call(
+            forward_kernel,
+            grid=(part,),
+            in_specs=[pl.BlockSpec(memory_space=pltpu.SMEM)]
+            + [cols(tok, skip)] * 3
+            + [cols(EDGE)] * 2
+            + [pl.BlockSpec((1, DH, DH), lambda h, skip=skip: (h + skip, 0, 0))],
+            out_specs=[cols(tok)] + saved_specs,
+            out_shape=[shape((tok, part * DH), BF16)] + saved,
+            scratch_shapes=[pltpu.VMEM((wide, DH), BF16)] * 2,
+            compiler_params=params,
+            cost_estimate=cost(24 * part * tok * SPAN * DH, 20 * tok * part * DH),
+            name="mixer_forward",
+        )(first, queries, keys, values, *halo[c], before)
+        mixed_parts.append(mixed_part)
+        kept.append(rest)
+    mixed = jnp.concatenate(mixed_parts, axis=1)
+
+    weight_terms = lax.dot_general(
+        grad_full, mixed, (((0,), (0,)), ((), ())), preferred_element_type=F32
+    ).astype(BF16)
+    weight, _ = lax.optimization_barrier((weight, weight_terms))
+    grad_mixed = mm_nt(grad_full, weight).astype(BF16)
+
+    back_parts = []
+    for c in range(count):
+        skip = c * part
+        back_parts.append(
+            pl.pallas_call(
+                backward_kernel,
+                grid=(part,),
+                in_specs=[cols(tok, skip)] * 3
+                + [cols(EDGE)] * 2
+                + [cols(tok, skip)]
+                + saved_specs,
+                out_specs=[cols(tok)] * 3 + [cols(EDGE)] * 2 + [heads(DH, DH)],
+                out_shape=[
+                    shape((tok, part * DH), BF16),
+                    shape((tok, part * DH), F32),
+                    shape((tok, part * DH), F32),
+                    shape((EDGE, part * DH), BF16),
+                    shape((EDGE, part * DH), BF16),
+                    shape((part, DH, DH), F32),
+                ],
+                scratch_shapes=[pltpu.VMEM((wide, DH), BF16)] * 2
+                + [pltpu.VMEM((wide, DH), F32)] * 2,
+                compiler_params=params,
+                cost_estimate=cost(24 * part * tok * SPAN * DH, 40 * tok * part * DH),
+                name="mixer_backward",
+            )(queries, keys, values, *halo[c], grad_mixed, *kept[c])
+        )
+    dq = jnp.concatenate([p[0] for p in back_parts], axis=1)
+    returned = [(shifted(p[3], -1), shifted(p[4], -1)) for p in back_parts]
+    weight_part = ring_scatter(weight_terms, {4: returned[0], 5: returned[1]})
+    projection_sensitivity = weight_part.T * tokens_all ** (-0.5)
+    later = entering(jnp.concatenate([p[5] for p in back_parts], axis=0), True)
+    mixed_late, _ = lax.optimization_barrier((mixed, back_parts[-1][5]))
+    mixer_result = lax.psum_scatter(
+        mm(mixed_late, weight).astype(BF16), "head", scatter_dimension=1, tiled=True
     )
-    projection_sensitivity = weight_part.T * tokens_all ** (-0.5)
-    grad_mixed = mm_nt(grad_full, weight).astype(BF16)
-    mixer_result = lax.psum_scatter(
-        mm(mixed, weight).astype(BF16), "head", scatter_dimension=1, tiled=True
-    )
-
-    dq, dk, dv, dke, dve, back = pl.pallas_call(
-        backward_kernel,
-        grid=(groups,),
-        in_specs=[cols(tok)] * 3 + [cols(EDGE)] * 2 + [cols(tok)] + saved_specs,
-        out_specs=[cols(tok)] * 3 + [cols(EDGE)] * 2 + [heads(DH, DH)],
-        out_shape=[
-            shape((tok, width), BF16),
-            shape((tok, width), F32),
-            shape((tok, width), F32),
-            shape((EDGE, width), BF16),
-            shape((EDGE, width), BF16),
-            shape((groups, DH, DH), F32),
-        ],
-        scratch_shapes=[pltpu.VMEM((wide, DH), BF16)] * 2 + [pltpu.VMEM((wide, DH), F32)] * 2,
-        compiler_params=params,
-        cost_estimate=cost(12 * groups * tok * SPAN * DH, 40 * tok * width),
-        name="mixer_backward",
-    )(queries, keys, values, ke, ve, grad_mixed, *kept)
-    rk = shifted(dke, -1)
-    rv = shifted(dve, -1)
-    later = entering(back, True)
-    gk, gv = pl.pallas_call(
-        finish_kernel,
-        grid=(groups,),
-        in_specs=[cols(tok)] * 4 + [cols(EDGE)] * 2 + [heads(DH, DH)],
-        out_specs=[cols(tok)] * 2,
-        out_shape=[shape((tok, width), BF16)] * 2,
-        compiler_params=params,
-        cost_estimate=cost(4 * tok * width * DH, 20 * tok * width),
-        name="mixer_finish",
-    )(keys, values, dk, dv, rk, rv, later)
+    done = []
+    for c in range(count):
+        skip = c * part
+        done.append(
+            pl.pallas_call(
+                finish_kernel,
+                grid=(part,),
+                in_specs=[cols(tok, skip)] * 2
+                + [cols(tok)] * 2
+                + [cols(EDGE)] * 2
+                + [pl.BlockSpec((1, DH, DH), lambda h, skip=skip: (h + skip, 0, 0))],
+                out_specs=[cols(tok)] * 2,
+                out_shape=[shape((tok, part * DH), BF16)] * 2,
+                compiler_params=params,
+                cost_estimate=cost(4 * tok * part * DH * DH, 20 * tok * part * DH),
+                name="mixer_finish",
+            )(keys, values, back_parts[c][1], back_parts[c][2], *returned[c], later)
+        )
+    gk = jnp.concatenate([d[0] for d in done], axis=1)
+    gv = jnp.concatenate([d[1] for d in done], axis=1)
     return (mixer_result, dq, gk, gv, projection_sensitivity)
 
 

time: 389 us -> 381 us (0.979)
  waiting for transfers between devices: 147 us -> 96.6 us
  starting transfers between devices: 78.8 us -> 117 us
  local copies, waits for them, and re-layouts: 46.2 us -> 56.4 us
  Pallas kernels: 45 us -> 39.3 us
    ppermute x28 -> x42, waiting for transfers between devices: 102 us -> 43 us  [ring_step(): return lax.ppermute(block, 'seq', pairs)]
    ppermute x28 -> x42, starting transfers between devices: 52.2 us -> 78 us  [ring_step(): return lax.ppermute(block, 'seq', pairs)]
    unnamed x38 -> x118, local copies, waits for them, and re-layouts: 12.8 us -> 27.7 us
    ppermute x10 -> x14, starting transfers between devices: 26.5 us -> 39.2 us  [shifted(): return lax.ppermute(shard, 'seq', pairs)]
    ppermute x10 -> x14, waiting for transfers between devices: 44.7 us -> 52.9 us  [shifted(): return lax.ppermute(shard, 'seq', pairs)]
    pallas_call x3 -> x6, Pallas kernels: 45 us -> 39.3 us  [the longest x2 19.1 us: shards(): pl.pallas_call(forward_kernel, grid=(part,), in_specs=[pl.BlockSpec(memor...]
    concatenate x0 -> x2, other arithmetic: none -> 3.92 us  [the longest x1 2.28 us: shards(): dq = jnp.concatenate([p[0] for p in back_parts], axis=1)]
    convert_element_type x6 -> x12, other arithmetic: 14.3 us -> 16.5 us  [ring_scatter(): sums[number] = total.astype(BF16) if t < count - 2 else total]
  transfers between devices with their start and end apart: 40 -> 58, of which waited for: 18 -> 26; matrix products, arithmetic and copies ran while one was open for 23% -> 15% of each run, Pallas kernels for 12% -> 8%
where the time goes in v3:
time: 381 us; the launch traced here: 379 us
  starting transfers between devices  117 us (31%)
  waiting for transfers between devices  96.6 us (25%)
  local copies, waits for them, and re-layouts  56.4 us (15%)
  Pallas kernels  39.3 us (10%)
  matrix products  28 us (7%)
  other arithmetic  26.8 us (7%)
  between operations  14.8 us (4%)
    ppermute x42, starting transfers between devices, ring_step(): return lax.ppermute(block, 'seq', pairs)  78 us
    ppermute x14, waiting for transfers between devices, shifted(): return lax.ppermute(shard, 'seq', pairs)  52.9 us
    ppermute x42, waiting for transfers between devices, ring_step(): return lax.ppermute(block, 'seq', pairs)  43 us
    ppermute x14, starting transfers between devices, shifted(): return lax.ppermute(shard, 'seq', pairs)  39.2 us
    unnamed x118, local copies, waits for them, and re-layouts  27.7 us
    pallas_call x2, Pallas kernels, shards(): pl.pallas_call(forward_kernel, grid=(part,), in_specs=[pl.BlockSpec(memor...  19.1 us
    convert_element_type x12, other arithmetic, ring_scatter(): sums[number] = total.astype(BF16) if t < count - 2 else total  16.5 us
    pallas_call x2, Pallas kernels, shards(): pl.pallas_call(backward_kernel, grid=(part,), in_specs=[cols(tok, skip)]...  16.4 us
  transfers between devices with their start and end apart: 58, of which 26 were waited for; matrix products, arithmetic and copies ran while one was open for 15% of the time, Pallas kernels for 8%

profile of v3, /device:TPU:0, one launch (start us, length us, event | category | flops | bytes accessed | tf_op | source)
XLA Modules:
  0.0 379.1 jit_solution(4520865094988721160)
XLA Ops:
  10.0 4.9 %collective-permute-start = (bf16[448,512]{1,0:T(8,128)(2,1)S(1)}, bf16[448,512]{1,0:T(8,128)(2,1)S(1)}, u32[]{:S(2)}, u32[]{:S(2)}) collective-permute-start(bf16[448,512]{1,0:T(8,128)(2,1)S(1)} %get-tuple-element.138), channel_id=1, source_target_pairs={{0,4},{4,8},{8,12},{12,16},{16,20},{20,24},{24,28},{1,5},{5,9},{9,... | collective-permute-start | bytes 1376264 | tf_op jit(solution)/shard_map/ppermute | solution.py:149
  31.4 5.5 %collective-permute-start.3 = (bf16[8,128,128]{2,1,0:T(8,128)(2,1)S(1)}, bf16[8,128,128]{2,1,0:T(8,128)(2,1)S(1)}, u32[]{:S(2)}, u32[]{:S(2)}) collective-permute-start(bf16[8,128,128]{2,1,0:T(8,128)(2,1)S(1)} %fusion.21), channel_id=1, source_target_pairs={{0,8},{4,12},{8,16},{12,20},{16,24},{20,28},{1,9},{5,13},{9,17},{1... | collective-permute-start | bytes 786440 | tf_op jit(solution)/shard_map/ppermute | solution.py:149
  36.9 14.3 %collective-permute-done.1.ve_ref = bf16[448,512]{1,0:T(8,128)(2,1)S(1)} collective-permute-done((bf16[448,512]{1,0:T(8,128)(2,1)S(1)}, bf16[448,512]{1,0:T(8,128)(2,1)S(1)}, u32[]{:S(2)}, u32[]{:S(2)}) %collective-permute-start.1) | collective-permute-done | bytes 458784 | tf_op jit(solution)/shard_map/ppermute | solution.py:149
  51.3 4.6 %collective-permute-start.9 = (bf16[512,512]{1,0:T(8,128)(2,1)S(1)}, bf16[512,512]{1,0:T(8,128)(2,1)}, u32[]{:S(2)}, u32[]{:S(2)}) collective-permute-start(bf16[512,512]{1,0:T(8,128)(2,1)S(1)} %collective-permute-done.7), channel_id=1, source_target_pairs={{0,8},{8,16},{16,24},{24,28},{28,20},{20,12},{12,4},{4,0},{1,9},{9... | collective-permute-start | bytes 1572872 | tf_op jit(solution)/shard_map/ppermute | solution.py:182
  56.0 5.0 %collective-permute-start.4 = (bf16[8,128,128]{2,1,0:T(8,128)(2,1)S(1)}, bf16[8,128,128]{2,1,0:T(8,128)(2,1)S(1)}, u32[]{:S(2)}, u32[]{:S(2)}) collective-permute-start(bf16[8,128,128]{2,1,0:T(8,128)(2,1)S(1)} %fusion.6), channel_id=1, source_target_pairs={{0,16},{4,20},{8,24},{12,28},{1,17},{5,21},{9,25},{13,29},{2,18},{... | collective-permute-start | bytes 786440 | tf_op jit(solution)/shard_map/ppermute | solution.py:149
  61.0 6.0 %collective-permute-start.5 = (bf16[448,512]{1,0:T(8,128)(2,1)}, bf16[448,512]{1,0:T(8,128)(2,1)S(1)}, u32[]{:S(2)}, u32[]{:S(2)}) collective-permute-start(bf16[448,512]{1,0:T(8,128)(2,1)} %get-tuple-element.137), channel_id=1, source_target_pairs={{0,4},{4,8},{8,12},{12,16},{16,20},{20,24},{24,28},{1,5},{5,9},{9,... | collective-permute-start | bytes 1376264 | tf_op jit(solution)/shard_map/ppermute | solution.py:149
  70.9 7.4 %collective-permute-done.5.ke_ref = bf16[448,512]{1,0:T(8,128)(2,1)S(1)} collective-permute-done((bf16[448,512]{1,0:T(8,128)(2,1)}, bf16[448,512]{1,0:T(8,128)(2,1)S(1)}, u32[]{:S(2)}, u32[]{:S(2)}) %collective-permute-start.5) | collective-permute-done | bytes 458784 | tf_op jit(solution)/shard_map/ppermute | solution.py:149
  79.1 5.7 %collective-permute-done.6.ve_ref = bf16[448,512]{1,0:T(8,128)(2,1)S(1)} collective-permute-done((bf16[448,512]{1,0:T(8,128)(2,1)S(1)}, bf16[448,512]{1,0:T(8,128)(2,1)S(1)}, u32[]{:S(2)}, u32[]{:S(2)}) %collective-permute-start.6) | collective-permute-done | bytes 458784 | tf_op jit(solution)/shard_map/ppermute | solution.py:149
  85.6 12.2 %collective-permute-start.11 = (bf16[512,512]{1,0:T(8,128)(2,1)}, bf16[512,512]{1,0:T(8,128)(2,1)}, u32[]{:S(2)}, u32[]{:S(2)}) collective-permute-start(bf16[512,512]{1,0:T(8,128)(2,1)} %collective-permute-done.9), channel_id=1, source_target_pairs={{0,8},{8,16},{16,24},{24,28},{28,20},{20,12},{12,4},{4,0},{1,9},{9... | collective-permute-start | bytes 1572872 | tf_op jit(solution)/shard_map/ppermute | solution.py:182
  103.2 5.1 %collective-permute-done.11 = bf16[512,512]{1,0:T(8,128)(2,1)} collective-permute-done((bf16[512,512]{1,0:T(8,128)(2,1)}, bf16[512,512]{1,0:T(8,128)(2,1)}, u32[]{:S(2)}, u32[]{:S(2)}) %collective-permute-start.11) | collective-permute-done | bytes 524320 | tf_op jit(solution)/shard_map/ppermute | solution.py:182
  108.4 7.2 %collective-permute-start.13 = (bf16[512,512]{1,0:T(8,128)(2,1)}, bf16[512,512]{1,0:T(8,128)(2,1)S(1)}, u32[]{:S(2)}, u32[]{:S(2)}) collective-permute-start(bf16[512,512]{1,0:T(8,128)(2,1)} %collective-permute-done.11), channel_id=1, source_target_pairs={{0,8},{8,16},{16,24},{24,28},{28,20},{20,12},{12,4},{4,0},{1,9},{9... | collective-permute-start | bytes 1572872 | tf_op jit(solution)/shard_map/ppermute | solution.py:182
  117.4 9.5 %mixer_forward.2 = (bf16[512,512]{1,0:T(8,128)(2,1)S(1)}, bf16[4,4,640,128]{3,2,1,0:T(8,128)(2,1)S(1)}, f32[4,4,128,128]{3,2,1,0:T(8,128)S(1)}, f32[4,4,128,128]...) custom-call(s32[1]{0:T(128)} %bitcast.first_ref, ...), custom_call_target="tpu_custom_call" | custom-call | flops 4026531840 | bytes 5242880 | tf_op jit(solution)/shard_map/mixer_forward/pallas_call | solution.py:282
  132.9 9.6 %mixer_forward.3 = (bf16[512,512]{1,0:T(8,128)(2,1)S(1)}, bf16[4,4,640,128]{3,2,1,0:T(8,128)(2,1)S(1)}, f32[4,4,128,128]{3,2,1,0:T(8,128)S(1)}, f32[4,4,128,128]...) custom-call(s32[1]{0:T(128)} %bitcast.first_ref, ...), custom_call_target="tpu_custom_call" | custom-call | flops 4026531840 | bytes 5242880 | tf_op jit(solution)/shard_map/mixer_forward/pallas_call | solution.py:282
  174.6 9.2 %convolution_convert_fusion = bf16[1024,4096]{1,0:T(8,128)(2,1)} fusion(bf16[512,1024]{1,0:T(8,128)(2,1)S(1)} %copy-done.55, bf16[512,4096]{1,0:T(8,128)(2,1)} %all-gather.2.cloned.1.call-done), kind=kOutput, calls=%fused_computation | convolution fusion | flops 4299161600 | bytes 13631488 | tf_op jit(solution)/shard_map/dot_general | solution.py:300
  183.8 7.2 %fusion.1.g_ref = bf16[512,1024]{1,0:T(8,128)(2,1)S(1)} fusion(bf16[1024,4096]{1,0:T(8,128)(2,1)} %constant_dynamic-update-slice_fusion.12, bf16[512,4096]{1,0:T(8,128)(2,1)S(1)} %copy-done.57), kind=kOutput, calls=%fused_computation.5 | convolution fusion | flops 4295491584 | bytes 13631488 | tf_op jit(solution)/shard_map/dot_general | solution.py:30
  191.2 8.3 %mixer_backward.2 = (bf16[512,512]{1,0:T(8,128)(2,1)S(1)}, f32[512,512]{1,0:T(8,128)S(1)}, f32[512,512]{1,0:T(8,128)S(1)}, bf16[448,512]{1,0:T(8,128)(2,1)S(1)},...) custom-call(bf16[512,1024]{1,0:T(8,128)(2,1)S(1)} %copy-done.15, bf16[512,1024]{1,0:T(8,128)(2,1)S(1)} %copy-done, ...), custom_call_target="tpu_custom_call" | custom-call | flops 4026531840 | bytes 10485760 | tf_op jit(solution)/shard_map/mixer_backward/pallas_call | solution.py:310
  202.8 9.4 %convolution_convert_fusion.1 = bf16[512,4096]{1,0:T(8,128)(2,1)} fusion(bf16[512,1024]{1,0:T(8,128)(2,1)S(1)} %copy-done.56, bf16[1024,4096]{1,0:T(8,128)(2,1)} %constant_dynamic-update-slice_fusion.12), kind=kOutput, calls=%fused_computation.1 | convolution fusion | flops 4297064448 | bytes 13631488 | tf_op jit(solution)/shard_map/dot_general | solution.py:26
  242.6 8.2 %mixer_backward.3 = (bf16[512,512]{1,0:T(8,128)(2,1)S(1)}, f32[512,512]{1,0:T(8,128)S(1)}, f32[512,512]{1,0:T(8,128)S(1)}, bf16[448,512]{1,0:T(8,128)(2,1)S(1)},...) custom-call(bf16[512,1024]{1,0:T(8,128)(2,1)S(1)} %copy-done.16, bf16[512,1024]{1,0:T(8,128)(2,1)S(1)} %copy-done, ...), custom_call_target="tpu_custom_call" | custom-call | flops 4026531840 | bytes 10485760 | tf_op jit(solution)/shard_map/mixer_backward/pallas_call | solution.py:310
  260.3 5.6 %collective-permute-done.34 = bf16[128,1024]{0,1:T(8,128)(2,1)S(1)} collective-permute-done((bf16[128,1024]{0,1:T(8,128)(2,1)S(1)}, bf16[128,1024]{0,1:T(8,128)(2,1)S(1)}, u32[]{:S(2)}, u32[]{:S(2)}) %collective-permute-start.34) | collective-permute-done | bytes 262176 | tf_op jit(solution)/shard_map/ppermute | solution.py:182
  285.7 7.1 %collective-permute-done.21.rk_ref = bf16[448,512]{1,0:T(8,128)(2,1)S(1)} collective-permute-done((bf16[448,512]{1,0:T(8,128)(2,1)S(1)}, bf16[448,512]{1,0:T(8,128)(2,1)S(1)}, u32[]{:S(2)}, u32[]{:S(2)}) %collective-permute-start.21) | collective-permute-done | bytes 458784 | tf_op jit(solution)/shard_map/ppermute | solution.py:149
  293.5 9.1 %collective-permute-done.22.rv_ref = bf16[448,512]{1,0:T(8,128)(2,1)S(1)} collective-permute-done((bf16[448,512]{1,0:T(8,128)(2,1)S(1)}, bf16[448,512]{1,0:T(8,128)(2,1)S(1)}, u32[]{:S(2)}, u32[]{:S(2)}) %collective-permute-start.22) | collective-permute-done | bytes 458784 | tf_op jit(solution)/shard_map/ppermute | solution.py:149
  322.2 7.9 %collective-permute-done.47 = bf16[128,1024]{0,1:T(8,128)(2,1)S(1)} collective-permute-done((bf16[128,1024]{0,1:T(8,128)(2,1)}, bf16[128,1024]{0,1:T(8,128)(2,1)S(1)}, u32[]{:S(2)}, u32[]{:S(2)}) %collective-permute-start.47) | collective-permute-done | bytes 262176 | tf_op jit(solution)/shard_map/ppermute | solution.py:182
  334.9 5.0 %collective-permute-start.50 = (bf16[128,1024]{0,1:T(8,128)(2,1)S(1)}, bf16[128,1024]{0,1:T(8,128)(2,1)S(1)}, u32[]{:S(2)}, u32[]{:S(2)}) collective-permute-start(bf16[128,1024]{0,1:T(8,128)(2,1)S(1)} %get-tuple-element.97), channel_id=1, source_target_pairs={{0,4},{8,0},{16,8},{24,16},{28,24},{20,28},{12,20},{4,12},{1,5},{9... | collective-permute-start | bytes 786440 | tf_op jit(solution)/shard_map/ppermute | solution.py:182
  342.2 4.6 %collective-permute-start.52 = (bf16[128,1024]{0,1:T(8,128)(2,1)S(1)}, bf16[128,1024]{0,1:T(8,128)(2,1)S(1)}, u32[]{:S(2)}, u32[]{:S(2)}) collective-permute-start(bf16[128,1024]{0,1:T(8,128)(2,1)S(1)} %get-tuple-element.98), channel_id=1, source_target_pairs={{0,8},{8,16},{16,24},{24,28},{28,20},{20,12},{12,4},{4,0},{1,9},{9... | collective-permute-start | bytes 786440 | tf_op jit(solution)/shard_map/ppermute | solution.py:182
  (268 shorter events, 185.7 us)
Async XLA Ops:
  7.2 167.4 %all-gather.2.cloned.1.call-start = ((), (), s32[]{:S(2)}) async-start(), calls=%async_computation.1 | async-start | bytes 5242880 | tf_op jit(solution)/shard_map/all_gather | solution.py:276
  7.9 364.3 %reduce-scatter.2.cloned.1.call-start = ((), (), s32[]{:S(2)}) async-start(), calls=%async_computation.2 | async-start | bytes 5242880 | tf_op jit(solution)/shard_map/reduce_scatter | solution.py:339
  10.0 27.0 %collective-permute-start = (bf16[448,512]{1,0:T(8,128)(2,1)S(1)}, bf16[448,512]{1,0:T(8,128)(2,1)S(1)}, u32[]{:S(2)}, u32[]{:S(2)}) collective-permute-start(bf16[448,512]{1,0:T(8,128)(2,1)S(1)} %get-tuple-element.138), channel_id=1, source_target_pairs={{0,4},{4,8},{8,12},{12,16},{16,20},{20,24},{24,28},{1,5},{5,9},{9,... | collective-permute-start | bytes 1376264 | tf_op jit(solution)/shard_map/ppermute | solution.py:149
  22.7 28.5 %collective-permute-start.7 = (bf16[512,512]{1,0:T(8,128)(2,1)S(1)}, bf16[512,512]{1,0:T(8,128)(2,1)S(1)}, u32[]{:S(2)}, u32[]{:S(2)}) collective-permute-start(bf16[512,512]{1,0:T(8,128)(2,1)S(1)} %get-tuple-element.134), channel_id=1, source_target_pairs={{0,8},{8,16},{16,24},{24,28},{28,20},{20,12},{12,4},{4,0},{1,9},{9... | collective-permute-start | bytes 1572872 | tf_op jit(solution)/shard_map/ppermute | solution.py:182
  24.4 26.9 %collective-permute-start.8 = (bf16[512,512]{1,0:T(8,128)(2,1)S(1)}, bf16[512,512]{1,0:T(8,128)(2,1)S(1)}, u32[]{:S(2)}, u32[]{:S(2)}) collective-permute-start(bf16[512,512]{1,0:T(8,128)(2,1)S(1)} %get-tuple-element.133), channel_id=1, source_target_pairs={{0,4},{8,0},{16,8},{24,16},{28,24},{20,28},{12,20},{4,12},{1,5},{9... | collective-permute-start | bytes 1572872 | tf_op jit(solution)/shard_map/ppermute | solution.py:182
  24.9 26.4 %collective-permute-start.1 = (bf16[448,512]{1,0:T(8,128)(2,1)S(1)}, bf16[448,512]{1,0:T(8,128)(2,1)S(1)}, u32[]{:S(2)}, u32[]{:S(2)}) collective-permute-start(bf16[448,512]{1,0:T(8,128)(2,1)S(1)} %get-tuple-element.136), channel_id=1, source_target_pairs={{0,4},{4,8},{8,12},{12,16},{16,20},{20,24},{24,28},{1,5},{5,9},{9,... | collective-permute-start | bytes 1376264 | tf_op jit(solution)/shard_map/ppermute | solution.py:149
  31.4 24.5 %collective-permute-start.3 = (bf16[8,128,128]{2,1,0:T(8,128)(2,1)S(1)}, bf16[8,128,128]{2,1,0:T(8,128)(2,1)S(1)}, u32[]{:S(2)}, u32[]{:S(2)}) collective-permute-start(bf16[8,128,128]{2,1,0:T(8,128)(2,1)S(1)} %fusion.21), channel_id=1, source_target_pairs={{0,8},{4,12},{8,16},{12,20},{16,24},{20,28},{1,9},{5,13},{9,17},{1... | collective-permute-start | bytes 786440 | tf_op jit(solution)/shard_map/ppermute | solution.py:149
  51.3 34.3 %collective-permute-start.9 = (bf16[512,512]{1,0:T(8,128)(2,1)S(1)}, bf16[512,512]{1,0:T(8,128)(2,1)}, u32[]{:S(2)}, u32[]{:S(2)}) collective-permute-start(bf16[512,512]{1,0:T(8,128)(2,1)S(1)} %collective-permute-done.7), channel_id=1, source_target_pairs={{0,8},{8,16},{16,24},{24,28},{28,20},{20,12},{12,4},{4,0},{1,9},{9... | collective-permute-start | bytes 1572872 | tf_op jit(solution)/shard_map/ppermute | solution.py:182
  55.9 29.6 %collective-permute-start.10 = (bf16[512,512]{1,0:T(8,128)(2,1)S(1)}, bf16[512,512]{1,0:T(8,128)(2,1)}, u32[]{:S(2)}, u32[]{:S(2)}) collective-permute-start(bf16[512,512]{1,0:T(8,128)(2,1)S(1)} %collective-permute-done.8), channel_id=1, source_target_pairs={{0,4},{8,0},{16,8},{24,16},{28,24},{20,28},{12,20},{4,12},{1,5},{9... | collective-permute-start | bytes 1572872 | tf_op jit(solution)/shard_map/ppermute | solution.py:182
  67.0 17.7 %collective-permute-start.6 = (bf16[448,512]{1,0:T(8,128)(2,1)S(1)}, bf16[448,512]{1,0:T(8,128)(2,1)S(1)}, u32[]{:S(2)}, u32[]{:S(2)}) collective-permute-start(bf16[448,512]{1,0:T(8,128)(2,1)S(1)} %get-tuple-element.135), channel_id=1, source_target_pairs={{0,4},{4,8},{8,12},{12,16},{16,20},{20,24},{24,28},{1,5},{5,9},{9,... | collective-permute-start | bytes 1376264 | tf_op jit(solution)/shard_map/ppermute | solution.py:149
  85.6 22.8 %collective-permute-start.11 = (bf16[512,512]{1,0:T(8,128)(2,1)}, bf16[512,512]{1,0:T(8,128)(2,1)}, u32[]{:S(2)}, u32[]{:S(2)}) collective-permute-start(bf16[512,512]{1,0:T(8,128)(2,1)} %collective-permute-done.9), channel_id=1, source_target_pairs={{0,8},{8,16},{16,24},{24,28},{28,20},{20,12},{12,4},{4,0},{1,9},{9... | collective-permute-start | bytes 1572872 | tf_op jit(solution)/shard_map/ppermute | solution.py:182
  97.7 18.7 %collective-permute-start.12 = (bf16[512,512]{1,0:T(8,128)(2,1)}, bf16[512,512]{1,0:T(8,128)(2,1)}, u32[]{:S(2)}, u32[]{:S(2)}) collective-permute-start(bf16[512,512]{1,0:T(8,128)(2,1)} %collective-permute-done.10), channel_id=1, source_target_pairs={{0,4},{8,0},{16,8},{24,16},{28,24},{20,28},{12,20},{4,12},{1,5},{9... | collective-permute-start | bytes 1572872 | tf_op jit(solution)/shard_map/ppermute | solution.py:182
  108.4 21.9 %collective-permute-start.13 = (bf16[512,512]{1,0:T(8,128)(2,1)}, bf16[512,512]{1,0:T(8,128)(2,1)S(1)}, u32[]{:S(2)}, u32[]{:S(2)}) collective-permute-start(bf16[512,512]{1,0:T(8,128)(2,1)} %collective-permute-done.11), channel_id=1, source_target_pairs={{0,8},{8,16},{16,24},{24,28},{28,20},{20,12},{12,4},{4,0},{1,9},{9... | collective-permute-start | bytes 1572872 | tf_op jit(solution)/shard_map/ppermute | solution.py:182
  132.8 18.8 %collective-permute-start.16 = (bf16[512,512]{1,0:T(8,128)(2,1)S(1)}, bf16[512,512]{1,0:T(8,128)(2,1)S(1)}, u32[]{:S(2)}, u32[]{:S(2)}) collective-permute-start(bf16[512,512]{1,0:T(8,128)(2,1)S(1)} %collective-permute-done.14), channel_id=1, source_target_pairs={{0,4},{8,0},{16,8},{24,16},{28,24},{20,28},{12,20},{4,12},{1,5},{9... | collective-permute-start | bytes 1572872 | tf_op jit(solution)/shard_map/ppermute | solution.py:182
  224.7 28.8 %collective-permute-start.29 = (bf16[128,1024]{0,1:T(8,128)(2,1)S(1)}, bf16[128,1024]{0,1:T(8,128)(2,1)S(1)}, u32[]{:S(2)}, u32[]{:S(2)}) collective-permute-start(bf16[128,1024]{0,1:T(8,128)(2,1)S(1)} %get-tuple-element.132), channel_id=1, source_target_pairs={{0,8},{8,16},{16,24},{24,28},{28,20},{20,12},{12,4},{4,0},{1,9},{9... | collective-permute-start | bytes 786440 | tf_op jit(solution)/shard_map/ppermute | solution.py:182
  226.8 26.7 %collective-permute-start.33 = (bf16[128,1024]{0,1:T(8,128)(2,1)S(1)}, bf16[128,1024]{0,1:T(8,128)(2,1)S(1)}, u32[]{:S(2)}, u32[]{:S(2)}) collective-permute-start(bf16[128,1024]{0,1:T(8,128)(2,1)S(1)} %get-tuple-element.131), channel_id=1, source_target_pairs={{0,4},{8,0},{16,8},{24,16},{28,24},{20,28},{12,20},{4,12},{1,5},{9... | collective-permute-start | bytes 786440 | tf_op jit(solution)/shard_map/ppermute | solution.py:182
  230.6 26.4 %collective-permute-start.41 = (bf16[128,1024]{0,1:T(8,128)(2,1)S(1)}, bf16[128,1024]{0,1:T(8,128)(2,1)S(1)}, u32[]{:S(2)}, u32[]{:S(2)}) collective-permute-start(bf16[128,1024]{0,1:T(8,128)(2,1)S(1)} %get-tuple-element.119), channel_id=1, source_target_pairs={{0,4},{8,0},{16,8},{24,16},{28,24},{20,28},{12,20},{4,12},{1,5},{9... | collective-permute-start | bytes 786440 | tf_op jit(solution)/shard_map/ppermute | solution.py:182
  231.2 25.8 %collective-permute-start.37 = (bf16[128,1024]{0,1:T(8,128)(2,1)S(1)}, bf16[128,1024]{0,1:T(8,128)(2,1)S(1)}, u32[]{:S(2)}, u32[]{:S(2)}) collective-permute-start(bf16[128,1024]{0,1:T(8,128)(2,1)S(1)} %get-tuple-element.120), channel_id=1, source_target_pairs={{0,8},{8,16},{16,24},{24,28},{28,20},{20,12},{12,4},{4,0},{1,9},{9... | collective-permute-start | bytes 786440 | tf_op jit(solution)/shard_map/ppermute | solution.py:182
  275.7 35.8 %collective-permute-start.23 = (bf16[8,128,128]{2,1,0:T(8,128)(2,1)}, bf16[8,128,128]{2,1,0:T(8,128)(2,1)S(1)}, u32[]{:S(2)}, u32[]{:S(2)}) collective-permute-start(bf16[8,128,128]{2,1,0:T(8,128)(2,1)} %convert_element_type.349), channel_id=1, source_target_pairs={{4,0},{8,4},{12,8},{16,12},{20,16},{24,20},{28,24},{5,1},{9,5},{13... | collective-permute-start | bytes 786440 | tf_op jit(solution)/shard_map/ppermute | solution.py:149
  279.3 23.3 %collective-permute-start.22 = (bf16[448,512]{1,0:T(8,128)(2,1)S(1)}, bf16[448,512]{1,0:T(8,128)(2,1)S(1)}, u32[]{:S(2)}, u32[]{:S(2)}) collective-permute-start(bf16[448,512]{1,0:T(8,128)(2,1)S(1)} %get-tuple-element.77), channel_id=1, source_target_pairs={{4,0},{8,4},{12,8},{16,12},{20,16},{24,20},{28,24},{5,1},{9,5},{13... | collective-permute-start | bytes 1376264 | tf_op jit(solution)/shard_map/ppermute | solution.py:149
  307.0 24.4 %collective-permute-start.26 = (bf16[448,512]{1,0:T(8,128)(2,1)}, bf16[448,512]{1,0:T(8,128)(2,1)S(1)}, u32[]{:S(2)}, u32[]{:S(2)}) collective-permute-start(bf16[448,512]{1,0:T(8,128)(2,1)} %copy-done.28), channel_id=1, source_target_pairs={{4,0},{8,4},{12,8},{16,12},{20,16},{24,20},{28,24},{5,1},{9,5},{13... | collective-permute-start | bytes 1376264 | tf_op jit(solution)/shard_map/ppermute | solution.py:149
  308.4 21.7 %collective-permute-start.47 = (bf16[128,1024]{0,1:T(8,128)(2,1)}, bf16[128,1024]{0,1:T(8,128)(2,1)S(1)}, u32[]{:S(2)}, u32[]{:S(2)}) collective-permute-start(bf16[128,1024]{0,1:T(8,128)(2,1)} %get-tuple-element.95), channel_id=1, source_target_pairs={{0,4},{8,0},{16,8},{24,16},{28,24},{20,28},{12,20},{4,12},{1,5},{9... | collective-permute-start | bytes 786440 | tf_op jit(solution)/shard_map/ppermute | solution.py:182
  311.5 18.6 %collective-permute-start.46 = (bf16[128,1024]{0,1:T(8,128)(2,1)}, bf16[128,1024]{0,1:T(8,128)(2,1)S(1)}, u32[]{:S(2)}, u32[]{:S(2)}) collective-permute-start(bf16[128,1024]{0,1:T(8,128)(2,1)} %get-tuple-element.93), channel_id=1, source_target_pairs={{0,8},{8,16},{16,24},{24,28},{28,20},{20,12},{12,4},{4,0},{1,9},{9... | collective-permute-start | bytes 786440 | tf_op jit(solution)/shard_map/ppermute | solution.py:182
  319.5 29.0 %collective-permute-start.24 = (bf16[8,128,128]{2,1,0:T(8,128)(2,1)S(1)}, bf16[8,128,128]{2,1,0:T(8,128)(2,1)S(1)}, u32[]{:S(2)}, u32[]{:S(2)}) collective-permute-start(bf16[8,128,128]{2,1,0:T(8,128)(2,1)S(1)} %fusion.22), channel_id=1, source_target_pairs={{8,0},{12,4},{16,8},{20,12},{24,16},{28,20},{9,1},{13,5},{17,9},{2... | collective-permute-start | bytes 786440 | tf_op jit(solution)/shard_map/ppermute | solution.py:149
  (92 other events, 1291.7 us)
Sparse Core Ops, SparseCore 0:
  9.6 37.1 all-gather.1
  212.4 43.4 reduce-scatter.1

commit v4 on v3

--- a/solution.py
+++ b/solution.py
@@ -192,8 +192,8 @@
     whole = lax.dynamic_update_slice(whole, block, (0, index * cols))
     up, down = block[:half], block[half:]
     for t in range(1, count):
-        if 2 <= t < 2 + len(after):
-            up, down, _ = lax.optimization_barrier((up, down, after[t - 2]))
+        if t in after:
+            up, down, _ = lax.optimization_barrier((up, down, after[t]))
         up = ring_step(up, 1)
         down = ring_step(down, -1)
         whole = lax.dynamic_update_slice(whole, up, (0, ring_owner(place - t, count) * cols))
@@ -201,30 +201,25 @@
     return whole
 
 
-def ring_scatter(parts, after):
+def ring_scatter(parts):
     count = lax.axis_size("seq")
     place = ring_place(lax.axis_index("seq"), count)
     rows = parts.shape[0] // count
-    part = rows // 4
-
-    def piece(at, number):
-        start = ring_owner(at, count) * rows + number * part
-        return lax.dynamic_slice_in_dim(parts, start, part, 0)
-
-    ways = (1, -1, 1, -1)
-    sums = [piece(place - way, number) for number, way in enumerate(ways)]
+    half = rows // 2
+
+    def piece(at, lower):
+        start = ring_owner(at, count) * rows + lower * half
+        return lax.dynamic_slice_in_dim(parts, start, half, 0)
+
+    up, down = piece(place - 1, 0), piece(place + 1, 1)
     for t in range(count - 1):
-        if t in after:
-            *sums, _ = lax.optimization_barrier((*sums, after[t]))
-        source = parts
-        for number, way in enumerate(ways):
-            arrived = ring_step(sums[number], way).astype(F32)
-            start = ring_owner(place - way * (2 + t), count) * rows + number * part
-            total = arrived + lax.dynamic_slice_in_dim(source, start, part, 0).astype(F32)
-            sums[number] = total.astype(BF16) if t < count - 2 else total
-            if number == 1 and t < count - 2:
-                source, _ = lax.optimization_barrier((parts, sums[0]))
-    return jnp.concatenate(sums, axis=0)
+        up = ring_step(up, 1).astype(F32) + piece(place - 2 - t, 0).astype(F32)
+        down = ring_step(down, -1).astype(F32) + piece(place + 2 + t, 1).astype(F32)
+        if t < count - 2:
+            up, down = up.astype(BF16), down.astype(BF16)
+        if t == 1:
+            early = (up, down)
+    return jnp.concatenate([up, down], axis=0), early
 
 
 def shards(queries, keys, values, w_out, grad_y):
@@ -274,7 +269,6 @@
         heads(tiles, DH, DH),
     ]
     grad_full = lax.all_gather(grad_y, "head", axis=1, tiled=True)
-    weight = ring_gather(w_out, [halo[0], (halo[1], before)])
 
     mixed_parts, kept = [], []
     for c in range(count):
@@ -300,7 +294,10 @@
     weight_terms = lax.dot_general(
         grad_full, mixed, (((0,), (0,)), ((), ())), preferred_element_type=F32
     ).astype(BF16)
-    weight, _ = lax.optimization_barrier((weight, weight_terms))
+    weight = ring_gather(w_out, {2: halo[0], 3: (halo[1], before), 5: weight_terms})
+    weight_part, early = ring_scatter(weight_terms)
+    weight, _ = lax.optimization_barrier((weight, early))
+    projection_sensitivity = weight_part.T * tokens_all ** (-0.5)
     grad_mixed = mm_nt(grad_full, weight).astype(BF16)
 
     back_parts = []
@@ -332,8 +329,6 @@
         )
     dq = jnp.concatenate([p[0] for p in back_parts], axis=1)
     returned = [(shifted(p[3], -1), shifted(p[4], -1)) for p in back_parts]
-    weight_part = ring_scatter(weight_terms, {4: returned[0], 5: returned[1]})
-    projection_sensitivity = weight_part.T * tokens_all ** (-0.5)
     later = entering(jnp.concatenate([p[5] for p in back_parts], axis=0), True)
     mixed_late, _ = lax.optimization_barrier((mixed, back_parts[-1][5]))
     mixer_result = lax.psum_scatter(

time: 381 us -> 371 us (0.974)
  waiting for transfers between devices: 96.6 us -> 139 us
  starting transfers between devices: 117 us -> 89.5 us
  local copies, waits for them, and re-layouts: 56.4 us -> 46.1 us
  matrix products: 28 us -> 20 us
  other arithmetic: 26.8 us -> 21 us
    ppermute x14, waiting for transfers between devices: 52.9 us -> 86.4 us  [shifted(): return lax.ppermute(shard, 'seq', pairs)]
    ppermute x42 -> x28, starting transfers between devices: 78 us -> 50.1 us  [ring_step(): return lax.ppermute(block, 'seq', pairs)]
    ppermute x42 -> x28, waiting for transfers between devices: 43 us -> 51.4 us  [ring_step(): return lax.ppermute(block, 'seq', pairs)]
    convert_element_type x12 -> x6, other arithmetic: 16.5 us -> 10.7 us  [ring_scatter(): up, down = (up.astype(BF16), down.astype(BF16))]
    unnamed x118 -> x128, local copies, waits for them, and re-layouts: 27.7 us -> 28.6 us
  transfers between devices with their start and end apart: 58 -> 44, of which waited for: 26 -> 19; matrix products, arithmetic and copies ran while one was open for 15% -> 13% of each run, Pallas kernels for 8% -> 8%
where the time goes in v4:
time: 371 us; the launch traced here: 370 us
  waiting for transfers between devices  139 us (37%)
  starting transfers between devices  89.5 us (24%)
  local copies, waits for them, and re-layouts  46.1 us (12%)
  Pallas kernels  39.3 us (11%)
  other arithmetic  21 us (6%)
  matrix products  20 us (5%)
  between operations  15.1 us (4%)
    ppermute x14, waiting for transfers between devices, shifted(): return lax.ppermute(shard, 'seq', pairs)  86.4 us
    ppermute x28, waiting for transfers between devices, ring_step(): return lax.ppermute(block, 'seq', pairs)  51.4 us
    ppermute x28, starting transfers between devices, ring_step(): return lax.ppermute(block, 'seq', pairs)  50.1 us
    ppermute x14, starting transfers between devices, shifted(): return lax.ppermute(shard, 'seq', pairs)  39.4 us
    unnamed x128, local copies, waits for them, and re-layouts  28.6 us
    pallas_call x2, Pallas kernels, shards(): pl.pallas_call(forward_kernel, grid=(part,), in_specs=[pl.BlockSpec(memor...  19.1 us
    pallas_call x2, Pallas kernels, shards(): pl.pallas_call(backward_kernel, grid=(part,), in_specs=[cols(tok, skip)]...  16.4 us
    convert_element_type x6, other arithmetic, ring_scatter(): up, down = (up.astype(BF16), down.astype(BF16))  10.7 us
  transfers between devices with their start and end apart: 44, of which 19 were waited for; matrix products, arithmetic and copies ran while one was open for 13% of the time, Pallas kernels for 8%

profile of v4, /device:TPU:0, one launch (start us, length us, event | category | flops | bytes accessed | tf_op | source)
XLA Modules:
  0.0 369.6 jit_solution(13541422557361583592)
XLA Ops:
  10.1 4.9 %collective-permute-start = (bf16[448,512]{1,0:T(8,128)(2,1)}, bf16[448,512]{1,0:T(8,128)(2,1)S(1)}, u32[]{:S(2)}, u32[]{:S(2)}) collective-permute-start(bf16[448,512]{1,0:T(8,128)(2,1)} %get-tuple-element.98), channel_id=1, source_target_pairs={{0,4},{4,8},{8,12},{12,16},{16,20},{20,24},{24,28},{1,5},{5,9},{9,... | collective-permute-start | bytes 1376264 | tf_op jit(solution)/shard_map/ppermute | solution.py:149
  31.8 5.5 %collective-permute-start.3 = (bf16[8,128,128]{2,1,0:T(8,128)(2,1)S(1)}, bf16[8,128,128]{2,1,0:T(8,128)(2,1)S(1)}, u32[]{:S(2)}, u32[]{:S(2)}) collective-permute-start(bf16[8,128,128]{2,1,0:T(8,128)(2,1)S(1)} %fusion.21), channel_id=1, source_target_pairs={{0,8},{4,12},{8,16},{12,20},{16,24},{20,28},{1,9},{5,13},{9,17},{1... | collective-permute-start | bytes 786440 | tf_op jit(solution)/shard_map/ppermute | solution.py:149
  37.3 14.3 %collective-permute-done.1.ve_ref = bf16[448,512]{1,0:T(8,128)(2,1)S(1)} collective-permute-done((bf16[448,512]{1,0:T(8,128)(2,1)S(1)}, bf16[448,512]{1,0:T(8,128)(2,1)S(1)}, u32[]{:S(2)}, u32[]{:S(2)}) %collective-permute-start.1) | collective-permute-done | bytes 458784 | tf_op jit(solution)/shard_map/ppermute | solution.py:149
  56.4 5.0 %collective-permute-start.4 = (bf16[8,128,128]{2,1,0:T(8,128)(2,1)S(1)}, bf16[8,128,128]{2,1,0:T(8,128)(2,1)S(1)}, u32[]{:S(2)}, u32[]{:S(2)}) collective-permute-start(bf16[8,128,128]{2,1,0:T(8,128)(2,1)S(1)} %fusion.18), channel_id=1, source_target_pairs={{0,16},{4,20},{8,24},{12,28},{1,17},{5,21},{9,25},{13,29},{2,18},{... | collective-permute-start | bytes 786440 | tf_op jit(solution)/shard_map/ppermute | solution.py:149
  61.4 6.0 %collective-permute-start.5 = (bf16[448,512]{1,0:T(8,128)(2,1)S(1)}, bf16[448,512]{1,0:T(8,128)(2,1)S(1)}, u32[]{:S(2)}, u32[]{:S(2)}) collective-permute-start(bf16[448,512]{1,0:T(8,128)(2,1)S(1)} %copy-done.59), channel_id=1, source_target_pairs={{0,4},{4,8},{8,12},{12,16},{16,20},{20,24},{24,28},{1,5},{5,9},{9,... | collective-permute-start | bytes 1376264 | tf_op jit(solution)/shard_map/ppermute | solution.py:149
  71.2 7.1 %collective-permute-done.5.ke_ref = bf16[448,512]{1,0:T(8,128)(2,1)S(1)} collective-permute-done((bf16[448,512]{1,0:T(8,128)(2,1)S(1)}, bf16[448,512]{1,0:T(8,128)(2,1)S(1)}, u32[]{:S(2)}, u32[]{:S(2)}) %collective-permute-start.5) | collective-permute-done | bytes 458784 | tf_op jit(solution)/shard_map/ppermute | solution.py:149
  79.1 6.0 %collective-permute-done.6.ve_ref = bf16[448,512]{1,0:T(8,128)(2,1)S(1)} collective-permute-done((bf16[448,512]{1,0:T(8,128)(2,1)S(1)}, bf16[448,512]{1,0:T(8,128)(2,1)S(1)}, u32[]{:S(2)}, u32[]{:S(2)}) %collective-permute-start.6) | collective-permute-done | bytes 458784 | tf_op jit(solution)/shard_map/ppermute | solution.py:149
  85.9 12.2 %collective-permute-start.11 = (bf16[512,512]{1,0:T(8,128)(2,1)}, bf16[512,512]{1,0:T(8,128)(2,1)}, u32[]{:S(2)}, u32[]{:S(2)}) collective-permute-start(bf16[512,512]{1,0:T(8,128)(2,1)} %collective-permute-done.9), channel_id=1, source_target_pairs={{0,8},{8,16},{16,24},{24,28},{28,20},{20,12},{12,4},{4,0},{1,9},{9... | collective-permute-start | bytes 1572872 | tf_op jit(solution)/shard_map/ppermute | solution.py:182
  99.5 9.2 %collective-permute-done.11 = bf16[512,512]{1,0:T(8,128)(2,1)} collective-permute-done((bf16[512,512]{1,0:T(8,128)(2,1)}, bf16[512,512]{1,0:T(8,128)(2,1)}, u32[]{:S(2)}, u32[]{:S(2)}) %collective-permute-start.11) | collective-permute-done | bytes 524320 | tf_op jit(solution)/shard_map/ppermute | solution.py:182
  108.7 7.2 %collective-permute-start.13 = (bf16[512,512]{1,0:T(8,128)(2,1)}, bf16[512,512]{1,0:T(8,128)(2,1)S(1)}, u32[]{:S(2)}, u32[]{:S(2)}) collective-permute-start(bf16[512,512]{1,0:T(8,128)(2,1)} %collective-permute-done.11), channel_id=1, source_target_pairs={{0,8},{8,16},{16,24},{24,28},{28,20},{20,12},{12,4},{4,0},{1,9},{9... | collective-permute-start | bytes 1572872 | tf_op jit(solution)/shard_map/ppermute | solution.py:182
  116.5 9.5 %mixer_forward.2 = (bf16[512,512]{1,0:T(8,128)(2,1)S(1)}, bf16[4,4,640,128]{3,2,1,0:T(8,128)(2,1)S(1)}, f32[4,4,128,128]{3,2,1,0:T(8,128)S(1)}, f32[4,4,128,128]...) custom-call(s32[1]{0:T(128)} %bitcast.first_ref, ...), custom_call_target="tpu_custom_call" | custom-call | flops 4026531840 | bytes 5242880 | tf_op jit(solution)/shard_map/mixer_forward/pallas_call | solution.py:276
  132.5 9.6 %mixer_forward.3 = (bf16[512,512]{1,0:T(8,128)(2,1)S(1)}, bf16[4,4,640,128]{3,2,1,0:T(8,128)(2,1)S(1)}, f32[4,4,128,128]{3,2,1,0:T(8,128)S(1)}, f32[4,4,128,128]...) custom-call(s32[1]{0:T(128)} %bitcast.first_ref, ...), custom_call_target="tpu_custom_call" | custom-call | flops 4026531840 | bytes 5242880 | tf_op jit(solution)/shard_map/mixer_forward/pallas_call | solution.py:276
  152.6 7.2 %convolution_convert_fusion = bf16[1024,4096]{1,0:T(8,128)(2,1)S(1)} fusion(bf16[512,1024]{1,0:T(8,128)(2,1)} %copy-done.60, bf16[512,4096]{1,0:T(8,128)(2,1)} %all-gather.2.cloned.1.call-done), kind=kOutput, calls=%fused_computation | convolution fusion | flops 4299161600 | bytes 13631488 | tf_op jit(solution)/shard_map/dot_general | solution.py:294
  169.7 8.9 %collective-permute-done.23 = bf16[256,1024]{0,1:T(8,128)(2,1)S(1)} collective-permute-done((bf16[256,1024]{0,1:T(8,128)(2,1)S(1)}, bf16[256,1024]{0,1:T(8,128)(2,1)S(1)}, u32[]{:S(2)}, u32[]{:S(2)}) %collective-permute-start.23) | collective-permute-done | bytes 524320 | tf_op jit(solution)/shard_map/ppermute | solution.py:182
  190.0 7.3 %collective-permute-done.24 = bf16[256,1024]{0,1:T(8,128)(2,1)S(1)} collective-permute-done((bf16[256,1024]{0,1:T(8,128)(2,1)S(1)}, bf16[256,1024]{0,1:T(8,128)(2,1)S(1)}, u32[]{:S(2)}, u32[]{:S(2)}) %collective-permute-start.24) | collective-permute-done | bytes 524320 | tf_op jit(solution)/shard_map/ppermute | solution.py:182
  203.3 8.2 %mixer_backward.2 = (bf16[512,512]{1,0:T(8,128)(2,1)S(1)}, f32[512,512]{1,0:T(8,128)S(1)}, f32[512,512]{1,0:T(8,128)S(1)}, bf16[448,512]{1,0:T(8,128)(2,1)S(1)},...) custom-call(bf16[512,1024]{1,0:T(8,128)(2,1)S(1)} %copy-done.11, bf16[512,1024]{1,0:T(8,128)(2,1)S(1)} %copy-done, ...), custom_call_target="tpu_custom_call" | custom-call | flops 4026531840 | bytes 10485760 | tf_op jit(solution)/shard_map/mixer_backward/pallas_call | solution.py:307
  215.0 6.0 %convolution_convert_fusion.1 = bf16[512,4096]{1,0:T(8,128)(2,1)} fusion(bf16[512,1024]{1,0:T(8,128)(2,1)S(1)} %copy-done.61, bf16[1024,4096]{1,0:T(8,128)(2,1)S(1)} %constant_dynamic-update-slice_fusion.12), kind=kOutput, calls=%fused_computation.1 | convolution fusion | flops 4297064448 | bytes 13631488 | tf_op jit(solution)/shard_map/dot_general | solution.py:26
  223.1 8.4 %collective-permute-done.32 = bf16[256,1024]{0,1:T(8,128)(2,1)} collective-permute-done((bf16[256,1024]{0,1:T(8,128)(2,1)}, bf16[256,1024]{0,1:T(8,128)(2,1)}, u32[]{:S(2)}, u32[]{:S(2)}) %collective-permute-start.32) | collective-permute-done | bytes 524320 | tf_op jit(solution)/shard_map/ppermute | solution.py:182
  237.8 7.7 %collective-permute-done.33 = bf16[256,1024]{0,1:T(8,128)(2,1)} collective-permute-done((bf16[256,1024]{0,1:T(8,128)(2,1)}, bf16[256,1024]{0,1:T(8,128)(2,1)}, u32[]{:S(2)}, u32[]{:S(2)}) %collective-permute-start.33) | collective-permute-done | bytes 524320 | tf_op jit(solution)/shard_map/ppermute | solution.py:182
  261.4 8.2 %mixer_backward.3 = (bf16[512,512]{1,0:T(8,128)(2,1)S(1)}, f32[512,512]{1,0:T(8,128)S(1)}, f32[512,512]{1,0:T(8,128)S(1)}, bf16[448,512]{1,0:T(8,128)(2,1)S(1)},...) custom-call(bf16[512,1024]{1,0:T(8,128)(2,1)S(1)} %copy-done.12, bf16[512,1024]{1,0:T(8,128)(2,1)S(1)} %copy-done, ...), custom_call_target="tpu_custom_call" | custom-call | flops 4026531840 | bytes 10485760 | tf_op jit(solution)/shard_map/mixer_backward/pallas_call | solution.py:307
  279.7 4.7 %collective-permute-done.27 = bf16[8,128,128]{2,1,0:T(8,128)(2,1)S(1)} collective-permute-done((bf16[8,128,128]{2,1,0:T(8,128)(2,1)S(1)}, bf16[8,128,128]{2,1,0:T(8,128)(2,1)S(1)}, u32[]{:S(2)}, u32[]{:S(2)}) %collective-permute-start.27) | collective-permute-done | bytes 262176 | tf_op jit(solution)/shard_map/ppermute | solution.py:149
  289.4 11.8 %collective-permute-done.28 = bf16[8,128,128]{2,1,0:T(8,128)(2,1)} collective-permute-done((bf16[8,128,128]{2,1,0:T(8,128)(2,1)}, bf16[8,128,128]{2,1,0:T(8,128)(2,1)}, u32[]{:S(2)}, u32[]{:S(2)}) %collective-permute-start.28) | collective-permute-done | bytes 262176 | tf_op jit(solution)/shard_map/ppermute | solution.py:149
  308.1 4.8 %collective-permute-start.36 = (bf16[256,1024]{0,1:T(8,128)(2,1)S(1)}, bf16[256,1024]{0,1:T(8,128)(2,1)S(1)}, u32[]{:S(2)}, u32[]{:S(2)}) collective-permute-start(bf16[256,1024]{0,1:T(8,128)(2,1)S(1)} %get-tuple-element.79), channel_id=1, source_target_pairs={{0,8},{8,16},{16,24},{24,28},{28,20},{20,12},{12,4},{4,0},{1,9},{9... | collective-permute-start | bytes 1572872 | tf_op jit(solution)/shard_map/ppermute | solution.py:182
  312.8 37.6 %collective-permute-done.29 = bf16[8,128,128]{2,1,0:T(8,128)(2,1)S(1)} collective-permute-done((bf16[8,128,128]{2,1,0:T(8,128)(2,1)S(1)}, bf16[8,128,128]{2,1,0:T(8,128)(2,1)S(1)}, u32[]{:S(2)}, u32[]{:S(2)}) %collective-permute-start.29) | collective-permute-done | bytes 262176 | tf_op jit(solution)/shard_map/ppermute | solution.py:149
  (244 shorter events, 137.2 us)
Async XLA Ops:
  7.2 145.4 %all-gather.2.cloned.1.call-start = ((), (), s32[]{:S(2)}) async-start(), calls=%async_computation.1 | async-start | bytes 5242880 | tf_op jit(solution)/shard_map/all_gather | solution.py:271
  7.9 354.8 %reduce-scatter.2.cloned.1.call-start = ((), (), s32[]{:S(2)}) async-start(), calls=%async_computation.2 | async-start | bytes 5242880 | tf_op jit(solution)/shard_map/reduce_scatter | solution.py:334
  10.1 27.2 %collective-permute-start = (bf16[448,512]{1,0:T(8,128)(2,1)}, bf16[448,512]{1,0:T(8,128)(2,1)S(1)}, u32[]{:S(2)}, u32[]{:S(2)}) collective-permute-start(bf16[448,512]{1,0:T(8,128)(2,1)} %get-tuple-element.98), channel_id=1, source_target_pairs={{0,4},{4,8},{8,12},{12,16},{16,20},{20,24},{24,28},{1,5},{5,9},{9,... | collective-permute-start | bytes 1376264 | tf_op jit(solution)/shard_map/ppermute | solution.py:149
  23.0 28.6 %collective-permute-start.7 = (bf16[512,512]{1,0:T(8,128)(2,1)S(1)}, bf16[512,512]{1,0:T(8,128)(2,1)S(1)}, u32[]{:S(2)}, u32[]{:S(2)}) collective-permute-start(bf16[512,512]{1,0:T(8,128)(2,1)S(1)} %get-tuple-element.94), channel_id=1, source_target_pairs={{0,8},{8,16},{16,24},{24,28},{28,20},{20,12},{12,4},{4,0},{1,9},{9... | collective-permute-start | bytes 1572872 | tf_op jit(solution)/shard_map/ppermute | solution.py:182
  24.7 27.0 %collective-permute-start.8 = (bf16[512,512]{1,0:T(8,128)(2,1)S(1)}, bf16[512,512]{1,0:T(8,128)(2,1)S(1)}, u32[]{:S(2)}, u32[]{:S(2)}) collective-permute-start(bf16[512,512]{1,0:T(8,128)(2,1)S(1)} %get-tuple-element.93), channel_id=1, source_target_pairs={{0,4},{8,0},{16,8},{24,16},{28,24},{20,28},{12,20},{4,12},{1,5},{9... | collective-permute-start | bytes 1572872 | tf_op jit(solution)/shard_map/ppermute | solution.py:182
  25.2 26.5 %collective-permute-start.1 = (bf16[448,512]{1,0:T(8,128)(2,1)S(1)}, bf16[448,512]{1,0:T(8,128)(2,1)S(1)}, u32[]{:S(2)}, u32[]{:S(2)}) collective-permute-start(bf16[448,512]{1,0:T(8,128)(2,1)S(1)} %get-tuple-element.96), channel_id=1, source_target_pairs={{0,4},{4,8},{8,12},{12,16},{16,20},{20,24},{24,28},{1,5},{5,9},{9,... | collective-permute-start | bytes 1376264 | tf_op jit(solution)/shard_map/ppermute | solution.py:149
  31.8 24.5 %collective-permute-start.3 = (bf16[8,128,128]{2,1,0:T(8,128)(2,1)S(1)}, bf16[8,128,128]{2,1,0:T(8,128)(2,1)S(1)}, u32[]{:S(2)}, u32[]{:S(2)}) collective-permute-start(bf16[8,128,128]{2,1,0:T(8,128)(2,1)S(1)} %fusion.21), channel_id=1, source_target_pairs={{0,8},{4,12},{8,16},{12,20},{16,24},{20,28},{1,9},{5,13},{9,17},{1... | collective-permute-start | bytes 786440 | tf_op jit(solution)/shard_map/ppermute | solution.py:149
  51.7 34.2 %collective-permute-start.9 = (bf16[512,512]{1,0:T(8,128)(2,1)S(1)}, bf16[512,512]{1,0:T(8,128)(2,1)}, u32[]{:S(2)}, u32[]{:S(2)}) collective-permute-start(bf16[512,512]{1,0:T(8,128)(2,1)S(1)} %collective-permute-done.7), channel_id=1, source_target_pairs={{0,8},{8,16},{16,24},{24,28},{28,20},{20,12},{12,4},{4,0},{1,9},{9... | collective-permute-start | bytes 1572872 | tf_op jit(solution)/shard_map/ppermute | solution.py:182
  56.3 29.6 %collective-permute-start.10 = (bf16[512,512]{1,0:T(8,128)(2,1)S(1)}, bf16[512,512]{1,0:T(8,128)(2,1)}, u32[]{:S(2)}, u32[]{:S(2)}) collective-permute-start(bf16[512,512]{1,0:T(8,128)(2,1)S(1)} %collective-permute-done.8), channel_id=1, source_target_pairs={{0,4},{8,0},{16,8},{24,16},{28,24},{20,28},{12,20},{4,12},{1,5},{9... | collective-permute-start | bytes 1572872 | tf_op jit(solution)/shard_map/ppermute | solution.py:182
  85.9 22.8 %collective-permute-start.11 = (bf16[512,512]{1,0:T(8,128)(2,1)}, bf16[512,512]{1,0:T(8,128)(2,1)}, u32[]{:S(2)}, u32[]{:S(2)}) collective-permute-start(bf16[512,512]{1,0:T(8,128)(2,1)} %collective-permute-done.9), channel_id=1, source_target_pairs={{0,8},{8,16},{16,24},{24,28},{28,20},{20,12},{12,4},{4,0},{1,9},{9... | collective-permute-start | bytes 1572872 | tf_op jit(solution)/shard_map/ppermute | solution.py:182
  108.7 21.7 %collective-permute-start.13 = (bf16[512,512]{1,0:T(8,128)(2,1)}, bf16[512,512]{1,0:T(8,128)(2,1)S(1)}, u32[]{:S(2)}, u32[]{:S(2)}) collective-permute-start(bf16[512,512]{1,0:T(8,128)(2,1)} %collective-permute-done.11), channel_id=1, source_target_pairs={{0,8},{8,16},{16,24},{24,28},{28,20},{20,12},{12,4},{4,0},{1,9},{9... | collective-permute-start | bytes 1572872 | tf_op jit(solution)/shard_map/ppermute | solution.py:182
  132.5 20.1 %collective-permute-start.16 = (bf16[512,512]{1,0:T(8,128)(2,1)S(1)}, bf16[512,512]{1,0:T(8,128)(2,1)}, u32[]{:S(2)}, u32[]{:S(2)}) collective-permute-start(bf16[512,512]{1,0:T(8,128)(2,1)S(1)} %collective-permute-done.14), channel_id=1, source_target_pairs={{0,4},{8,0},{16,8},{24,16},{28,24},{20,28},{12,20},{4,12},{1,5},{9... | collective-permute-start | bytes 1572872 | tf_op jit(solution)/shard_map/ppermute | solution.py:182
  167.6 19.2 %collective-permute-start.19 = (bf16[512,512]{1,0:T(8,128)(2,1)}, bf16[512,512]{1,0:T(8,128)(2,1)S(1)}, u32[]{:S(2)}, u32[]{:S(2)}) collective-permute-start(bf16[512,512]{1,0:T(8,128)(2,1)} %collective-permute-done.17), channel_id=1, source_target_pairs={{0,8},{8,16},{16,24},{24,28},{28,20},{20,12},{12,4},{4,0},{1,9},{9... | collective-permute-start | bytes 1572872 | tf_op jit(solution)/shard_map/ppermute | solution.py:182
  169.7 20.2 %collective-permute-start.20 = (bf16[512,512]{1,0:T(8,128)(2,1)}, bf16[512,512]{1,0:T(8,128)(2,1)S(1)}, u32[]{:S(2)}, u32[]{:S(2)}) collective-permute-start(bf16[512,512]{1,0:T(8,128)(2,1)} %collective-permute-done.18), channel_id=1, source_target_pairs={{0,4},{8,0},{16,8},{24,16},{28,24},{20,28},{12,20},{4,12},{1,5},{9... | collective-permute-start | bytes 1572872 | tf_op jit(solution)/shard_map/ppermute | solution.py:182
  249.5 25.0 %collective-permute-start.34 = (bf16[256,1024]{0,1:T(8,128)(2,1)S(1)}, bf16[256,1024]{0,1:T(8,128)(2,1)S(1)}, u32[]{:S(2)}, u32[]{:S(2)}) collective-permute-start(bf16[256,1024]{0,1:T(8,128)(2,1)S(1)} %get-tuple-element.83), channel_id=1, source_target_pairs={{0,8},{8,16},{16,24},{24,28},{28,20},{20,12},{12,4},{4,0},{1,9},{9... | collective-permute-start | bytes 1572872 | tf_op jit(solution)/shard_map/ppermute | solution.py:182
  250.4 24.1 %collective-permute-start.39 = (bf16[256,1024]{0,1:T(8,128)(2,1)S(1)}, bf16[256,1024]{0,1:T(8,128)(2,1)S(1)}, u32[]{:S(2)}, u32[]{:S(2)}) collective-permute-start(bf16[256,1024]{0,1:T(8,128)(2,1)S(1)} %get-tuple-element.84), channel_id=1, source_target_pairs={{0,4},{8,0},{16,8},{24,16},{28,24},{20,28},{12,20},{4,12},{1,5},{9... | collective-permute-start | bytes 1572872 | tf_op jit(solution)/shard_map/ppermute | solution.py:182
  277.0 26.6 %collective-permute-start.35 = (bf16[256,1024]{0,1:T(8,128)(2,1)}, bf16[256,1024]{0,1:T(8,128)(2,1)}, u32[]{:S(2)}, u32[]{:S(2)}) collective-permute-start(bf16[256,1024]{0,1:T(8,128)(2,1)} %get-tuple-element.81), channel_id=1, source_target_pairs={{0,8},{8,16},{16,24},{24,28},{28,20},{20,12},{12,4},{4,0},{1,9},{9... | collective-permute-start | bytes 1572872 | tf_op jit(solution)/shard_map/ppermute | solution.py:182
  279.5 25.5 %collective-permute-start.40 = (bf16[256,1024]{0,1:T(8,128)(2,1)}, bf16[256,1024]{0,1:T(8,128)(2,1)}, u32[]{:S(2)}, u32[]{:S(2)}) collective-permute-start(bf16[256,1024]{0,1:T(8,128)(2,1)} %get-tuple-element.82), channel_id=1, source_target_pairs={{0,4},{8,0},{16,8},{24,16},{28,24},{20,28},{12,20},{4,12},{1,5},{9... | collective-permute-start | bytes 1572872 | tf_op jit(solution)/shard_map/ppermute | solution.py:182
  286.5 21.6 %collective-permute-start.30 = (bf16[448,512]{1,0:T(8,128)(2,1)}, bf16[448,512]{1,0:T(8,128)(2,1)S(1)}, u32[]{:S(2)}, u32[]{:S(2)}) collective-permute-start(bf16[448,512]{1,0:T(8,128)(2,1)} %copy-done.24), channel_id=1, source_target_pairs={{4,0},{8,4},{12,8},{16,12},{20,16},{24,20},{28,24},{5,1},{9,5},{13... | collective-permute-start | bytes 1376264 | tf_op jit(solution)/shard_map/ppermute | solution.py:149
  288.1 65.7 %collective-permute-start.31 = (bf16[448,512]{1,0:T(8,128)(2,1)}, bf16[448,512]{1,0:T(8,128)(2,1)S(1)}, u32[]{:S(2)}, u32[]{:S(2)}) collective-permute-start(bf16[448,512]{1,0:T(8,128)(2,1)} %copy-done.23), channel_id=1, source_target_pairs={{4,0},{8,4},{12,8},{16,12},{20,16},{24,20},{28,24},{5,1},{9,5},{13... | collective-permute-start | bytes 1376264 | tf_op jit(solution)/shard_map/ppermute | solution.py:149
  301.1 54.6 %collective-permute-start.25 = (bf16[448,512]{1,0:T(8,128)(2,1)}, bf16[448,512]{1,0:T(8,128)(2,1)S(1)}, u32[]{:S(2)}, u32[]{:S(2)}) collective-permute-start(bf16[448,512]{1,0:T(8,128)(2,1)} %copy-done.26), channel_id=1, source_target_pairs={{4,0},{8,4},{12,8},{16,12},{20,16},{24,20},{28,24},{5,1},{9,5},{13... | collective-permute-start | bytes 1376264 | tf_op jit(solution)/shard_map/ppermute | solution.py:149
  303.6 52.1 %collective-permute-start.26 = (bf16[448,512]{1,0:T(8,128)(2,1)}, bf16[448,512]{1,0:T(8,128)(2,1)S(1)}, u32[]{:S(2)}, u32[]{:S(2)}) collective-permute-start(bf16[448,512]{1,0:T(8,128)(2,1)} %copy-done.25), channel_id=1, source_target_pairs={{4,0},{8,4},{12,8},{16,12},{20,16},{24,20},{28,24},{5,1},{9,5},{13... | collective-permute-start | bytes 1376264 | tf_op jit(solution)/shard_map/ppermute | solution.py:149
  305.0 45.5 %collective-permute-start.29 = (bf16[8,128,128]{2,1,0:T(8,128)(2,1)S(1)}, bf16[8,128,128]{2,1,0:T(8,128)(2,1)S(1)}, u32[]{:S(2)}, u32[]{:S(2)}) collective-permute-start(bf16[8,128,128]{2,1,0:T(8,128)(2,1)S(1)} %fusion.20), channel_id=1, source_target_pairs={{16,0},{20,4},{24,8},{28,12},{17,1},{21,5},{25,9},{29,13},{18,2},{... | collective-permute-start | bytes 786440 | tf_op jit(solution)/shard_map/ppermute | solution.py:149
  308.1 51.2 %collective-permute-start.36 = (bf16[256,1024]{0,1:T(8,128)(2,1)S(1)}, bf16[256,1024]{0,1:T(8,128)(2,1)S(1)}, u32[]{:S(2)}, u32[]{:S(2)}) collective-permute-start(bf16[256,1024]{0,1:T(8,128)(2,1)S(1)} %get-tuple-element.79), channel_id=1, source_target_pairs={{0,8},{8,16},{16,24},{24,28},{28,20},{20,12},{12,4},{4,0},{1,9},{9... | collective-permute-start | bytes 1572872 | tf_op jit(solution)/shard_map/ppermute | solution.py:182
  (83 other events, 1278.7 us)
Sparse Core Ops, SparseCore 0:
  9.6 37.1 all-gather.1
  221.2 42.9 reduce-scatter.1
